TPU v7x, 1024 devices: a whole 4x8x16 slice. The times are simulated.
1024 devices in a mesh: px: 64 (over y, x, core), py: 16 (over z).
Axes of the slice: x: 4, y: 8, z: 16, core: 2. Of those that a mesh axis runs over, the one named last changes fastest.
Arguments:
- velocity: float32 [2, 20, 128, 2048], P(None, None, 'px', 'py'), may hold values from -6 to 6
- direction: float32 [2, 20, 128, 2048], P(None, None, 'px', 'py'), may hold values from -2 to 2
- forcing: float32 [2, 20, 128, 2048], P(None, None, 'px', 'py'), may hold values from -6 to 6
- softness: float32 [128, 2048], P('px', 'py'), may hold values from 0.5 to 2
- friction: float32 [128, 2048], P('px', 'py'), may hold values from 0.3 to 3
- links: int32 [4, 128, 2048], P(None, 'px', 'py'), may hold values from 0 to 8
- aggregate: int32 [128, 2048], P('px', 'py'), may hold values from 0 to 63
- coarse_diag: float32 [65536], P('px'), may hold values from 1 to 3
- coarse_vals: float32 [4, 65536], P(None, 'px'), may hold values from -0.2 to 0.2
- coarse_cols: int32 [4, 65536], P(None, 'px'), may hold values from 0 to 1023
Outputs:
- image: float32 [2, 20, 128, 2048], P(None, None, 'px', 'py')
- answer: float32 [2, 20, 128, 2048], P(None, None, 'px', 'py')
Inputs may be any that keep to these rules, and one draw needn't show every extreme that they name: `links`: 0 to 7 name one of the eight surrounding columns in the order of the steps, 8 an unused slot; a column may name a direction twice. `aggregate`: ids are local to a device. `coarse_cols`: numbers count the aggregates of one subgroup.
All inputs are finite; a program needn't handle non-finite values.
Results may differ from a plain program's by a relative error of at most 0.00029.
Values sent between devices are 32-bit elements; how exact they have to be, the bound alone decides.
A program may use at most 32 MiB of HBM per device.

v0:
```python
import jax
import jax.numpy as jnp
from jax import lax
from jax.sharding import PartitionSpec as P

CITERS = 4
AGG_DEV = 64


KZ = 4.0
EPS0 = 0.05
OMEGA = 0.8
OFFSETS = ((-1, -1), (-1, 0), (-1, 1), (0, -1), (0, 1), (1, -1), (1, 0), (1, 1))


def extended_2(cells, sides, width):
    for axis, dim in sides:
        count = lax.axis_size(axis)
        ends = count - 1
        head = lax.slice_in_dim(cells, 0, width, axis=dim)
        tail = lax.slice_in_dim(cells, cells.shape[dim] - width, cells.shape[dim], axis=dim)
        cells = jnp.concatenate(
            [
                lax.ppermute(tail, axis, [(i, (i + 1) % count) for i in range(ends)]),
                cells,
                lax.ppermute(head, axis, [((i + 1) % count, i) for i in range(ends)]),
            ],
            axis=dim,
        )
    return cells


def link_counts(links):
    codes = jnp.arange(8, dtype=jnp.int32)
    return jnp.sum((links[None] == codes[:, None, None, None]).astype(jnp.float32), axis=1)


def viscosity(field, rate):
    above = jnp.concatenate([field[:, 1:], field[:, -1:]], axis=1)
    below = jnp.concatenate([field[:, :1], field[:, :-1]], axis=1)
    shear = above - below
    strain = EPS0 + 0.25 * KZ * jnp.sum(shear * shear, axis=0)
    return rate * jnp.power(strain, -1.0 / 3.0)


def neighbours(extended, shift_x, shift_y):
    height = extended.shape[-2] - 2
    width = extended.shape[-1] - 2
    return extended[..., 1 + shift_x : 1 + shift_x + height, 1 + shift_y : 1 + shift_y + width]


def operator(field_ext, rate_ext, friction, counts):
    eta_ext = viscosity(field_ext, rate_ext)
    field = neighbours(field_ext, 0, 0)
    eta = neighbours(eta_ext, 0, 0)
    face = 0.5 * (eta[:-1] + eta[1:])
    flux = KZ * face * (field[:, 1:] - field[:, :-1])
    empty = jnp.zeros_like(flux[:, :1])
    result = jnp.concatenate([empty, flux], axis=1) - jnp.concatenate([flux, empty], axis=1)
    result = result + jnp.concatenate(
        [friction * field[:, :1], jnp.zeros_like(field[:, 1:])], axis=1
    )
    for number, (shift_x, shift_y) in enumerate(OFFSETS):
        coupling = counts[number] * 0.5 * (eta + neighbours(eta_ext, shift_x, shift_y))
        result = result + coupling * (field - neighbours(field_ext, shift_x, shift_y))
    return result


def line_factors(eta_ext, friction, counts):
    eta = neighbours(eta_ext, 0, 0)
    depth = eta.shape[0]
    face = 0.5 * (eta[:-1] + eta[1:])
    side = jnp.zeros_like(eta)
    for number, (shift_x, shift_y) in enumerate(OFFSETS):
        side = side + counts[number] * 0.5 * (eta + neighbours(eta_ext, shift_x, shift_y))
    lowers, pivots, ratios = ([], [], [])
    for level in range(depth):
        middle = side[level]
        if level > 0:
            middle = middle + KZ * face[level - 1]
        if level < depth - 1:
            middle = middle + KZ * face[level]
        if level == 0:
            middle = middle + friction
            lowers.append(jnp.zeros_like(middle))
            pivot = middle
        else:
            lower = -KZ * face[level - 1]
            lowers.append(lower)
            pivot = middle - lower * ratios[level - 1]
        pivots.append(pivot)
        if level < depth - 1:
            ratios.append(-KZ * face[level] / pivot)
        else:
            ratios.append(jnp.zeros_like(pivot))
    return (lowers, pivots, ratios)


def line_solve(factors, rhs):
    lowers, pivots, ratios = factors
    depth = len(pivots)
    forward = [rhs[:, 0] / pivots[0]]
    for level in range(1, depth):
        forward.append((rhs[:, level] - lowers[level] * forward[level - 1]) / pivots[level])
    backward = [None] * depth
    backward[depth - 1] = forward[depth - 1]
    for level in range(depth - 2, -1, -1):
        backward[level] = forward[level] - ratios[level] * backward[level + 1]
    return jnp.stack(backward, axis=1)


def jacobi_sweep(mine, whole, target, diag, vals, cols):
    applied = diag * mine
    for slot in range(vals.shape[0]):
        applied = applied + vals[slot] * whole[:, cols[slot]]
    return mine + OMEGA * (target - applied) / diag


def body(
    velocity,
    direction,
    forcing,
    softness,
    friction,
    links,
    aggregate,
    coarse_diag,
    coarse_vals,
    coarse_cols,
):
    comps, layers, height, width = velocity.shape
    depth = comps * layers
    counts = link_counts(links)
    stacked = jnp.concatenate(
        [
            velocity.reshape(depth, height, width),
            direction.reshape(depth, height, width),
            softness[None],
        ],
        axis=0,
    )
    extended = extended_2(stacked, (("px", 1), ("py", 2)), 1)
    state_ext = extended[:depth].reshape(comps, layers, height + 2, width + 2)
    probe_ext = extended[depth : 2 * depth].reshape(comps, layers, height + 2, width + 2)
    rate_ext = extended[2 * depth]

    def apply_op(field_ext):
        return operator(field_ext, rate_ext, friction, counts)

    def jacobian(step_ext):
        return jax.jvp(apply_op, (state_ext,), (step_ext,))[1]

    image = jacobian(probe_ext)
    resid = forcing - image
    factors = line_factors(viscosity(state_ext, rate_ext), friction, counts)
    smooth = line_solve(factors, resid)
    smooth_ext = extended_2(smooth, (("px", 2), ("py", 3)), 1)
    after = resid - jacobian(smooth_ext)
    column_mean = jnp.sum(after, axis=1) / layers
    restricted = jax.ops.segment_sum(
        column_mean.reshape(comps, -1).T, aggregate.reshape(-1), num_segments=AGG_DEV
    ).T
    start = lax.axis_index("py") * AGG_DEV
    whole = lax.all_gather(restricted, "py", axis=1, tiled=True)
    iterate = jnp.zeros_like(whole)
    for sweep in range(CITERS):
        iterate = jacobi_sweep(iterate, iterate, whole, coarse_diag, coarse_vals, coarse_cols)
    owned = lax.dynamic_slice_in_dim(iterate, start, AGG_DEV, 1)
    correction = owned[:, aggregate]
    coarse_step = smooth + correction[:, None]
    coarse_ext = extended_2(coarse_step, (("px", 2), ("py", 3)), 1)
    final = resid - jacobian(coarse_ext)
    answer = coarse_step + line_solve(factors, final)
    return (image, answer)


def solution(mesh):
    return jax.shard_map(
        body,
        mesh=mesh,
        in_specs=(
            P(None, None, "px", "py"),
            P(None, None, "px", "py"),
            P(None, None, "px", "py"),
            P("px", "py"),
            P("px", "py"),
            P(None, "px", "py"),
            P("px", "py"),
            P("px"),
            P(None, "px"),
            P(None, "px"),
        ),
        out_specs=(P(None, None, "px", "py"), P(None, None, "px", "py")),
        check_vma=False,
    )
```

profile of v0, /device:TPU:31, one launch (start us, length us, event | category | flops | bytes accessed | tf_op | source)
XLA Modules:
  0.0 168.6 jit_solution(9833705796699301416)
XLA Ops:
  0.6 0.7 copy-done.7
  1.3 0.8 pad_maximum_fusion.16
  2.2 4.9 %collective-permute-start = (f32[81,1,128]{2,1,0:T(1,128)S(1)}, f32[81,1,128]{2,1,0:T(1,128)S(1)}, u32[]{:S(2)}, u32[]{:S(2)}) collective-permute-start(f32[81,1,128]{2,1,0:T(1,128)S(1)} %get-tuple-element.138), channel_id=1, source_target_pairs={{0,16},{16,32},{32,48},{48,64},{64,80},{80,96},{96,112},{112,128},... | collective-permute-start | bytes 124424 | tf_op jit(solution)/shard_map/ppermute | solution.py:24
  7.1 1.9 %collective-permute-start.1 = (f32[81,1,128]{2,1,0:T(1,128)S(1)}, f32[81,1,128]{2,1,0:T(1,128)S(1)}, u32[]{:S(2)}, u32[]{:S(2)}) collective-permute-start(f32[81,1,128]{2,1,0:T(1,128)S(1)} %get-tuple-element.139), channel_id=1, source_target_pairs={{16,0},{32,16},{48,32},{64,48},{80,64},{96,80},{112,96},{128,112},... | collective-permute-start | bytes 124424 | tf_op jit(solution)/shard_map/ppermute | solution.py:26
  9.2 0.6 copy-done.49
  9.9 0.6 pad_clamp_fusion
  10.5 5.3 %collective-permute-done.1 = f32[81,1,128]{2,1,0:T(1,128)S(1)} collective-permute-done((f32[81,1,128]{2,1,0:T(1,128)S(1)}, f32[81,1,128]{2,1,0:T(1,128)S(1)}, u32[]{:S(2)}, u32[]{:S(2)}) %collective-permute-start.1) | collective-permute-done | bytes 41504 | tf_op jit(solution)/shard_map/ppermute | solution.py:26
  16.1 4.0 %collective-permute-start.2 = (f32[81,4,1]{2,1,0:T(4,128)S(1)}, f32[81,4,1]{2,1,0:T(4,128)S(1)}, u32[]{:S(2)}, u32[]{:S(2)}) collective-permute-start(f32[81,4,1]{2,1,0:T(4,128)S(1)} %get-tuple-element.122), channel_id=1, source_target_pairs={{0,1},{1,2},{2,3},{3,4},{4,5},{5,6},{6,7},{7,8},{8,9},{9,10},{10,1... | collective-permute-start | bytes 3896 | tf_op jit(solution)/shard_map/ppermute | solution.py:24
  20.1 1.3 collective-permute-start.3
  21.4 0.9 collective-permute-done.2
  22.3 4.5 %collective-permute-done.3 = f32[81,4,1]{2,1,0:T(4,128)S(1)} collective-permute-done((f32[81,4,1]{2,1,0:T(4,128)S(1)}, f32[81,4,1]{2,1,0:T(4,128)S(1)}, u32[]{:S(2)}, u32[]{:S(2)}) %collective-permute-start.3) | collective-permute-done | bytes 1328 | tf_op jit(solution)/shard_map/ppermute | solution.py:26
  26.8 0.7 pad_maximum_fusion.9
  27.6 0.2 fusion.28
  27.9 0.2 multiply_multiply_fusion.2
  28.5 0.2 add_add_fusion
  28.8 0.5 copy-done.4
  29.9 0.2 fusion.117
  30.1 0.5 copy-done.3
  30.6 1.2 fusion.360
  32.6 3.0 %collective-permute-start.4 = (f32[2,20,1,128]{3,2,1,0:T(1,128)S(1)}, f32[2,20,1,128]{3,2,1,0:T(1,128)S(1)}, u32[]{:S(2)}, u32[]{:S(2)}) collective-permute-start(f32[2,20,1,128]{3,2,1,0:T(1,128)S(1)} %get-tuple-element.172), channel_id=1, source_target_pairs={{0,16},{16,32},{32,48},{48,64},{64,80},{80,96},{96,112},{112,128},... | collective-permute-start | bytes 61448 | tf_op jit(solution)/shard_map/ppermute | solution.py:24
  35.6 1.9 %collective-permute-start.5 = (f32[2,20,1,128]{3,2,1,0:T(1,128)S(1)}, f32[2,20,1,128]{3,2,1,0:T(1,128)S(1)}, u32[]{:S(2)}, u32[]{:S(2)}) collective-permute-start(f32[2,20,1,128]{3,2,1,0:T(1,128)S(1)} %get-tuple-element.173), channel_id=1, source_target_pairs={{16,0},{32,16},{48,32},{64,48},{80,64},{96,80},{112,96},{128,112},... | collective-permute-start | bytes 61448 | tf_op jit(solution)/shard_map/ppermute | solution.py:26
  37.6 2.8 %gather_fusion.1 = f32[1024,2]{1,0:T(8,128)S(1)} fusion(f32[2,1024]{0,1:T(8,128)S(1)} %broadcast_in_dim.13, s32[1024]{0:T(1024)S(1)} %get-tuple-element.274), kind=kCustom, calls=%fused_computation.1 | custom fusion | bytes 20480 | tf_op jit(solution)/shard_map/gather | solution.py:115
  40.6 2.8 %gather_fusion.2 = f32[1024,2]{1,0:T(8,128)S(1)} fusion(f32[2,1024]{0,1:T(8,128)S(1)} %broadcast_in_dim.13, s32[1024]{0:T(1024)S(1)} %get-tuple-element.273), kind=kCustom, calls=%fused_computation.2 | custom fusion | bytes 20480 | tf_op jit(solution)/shard_map/gather | solution.py:115
  43.6 2.8 %gather_fusion.3 = f32[1024,2]{1,0:T(8,128)S(1)} fusion(f32[2,1024]{0,1:T(8,128)S(1)} %broadcast_in_dim.13, s32[1024]{0:T(1024)S(1)} %get-tuple-element.272), kind=kCustom, calls=%fused_computation.3 | custom fusion | bytes 20480 | tf_op jit(solution)/shard_map/gather | solution.py:115
  46.6 2.8 %gather_fusion = f32[1024,2]{1,0:T(8,128)S(1)} fusion(f32[2,1024]{0,1:T(8,128)S(1)} %broadcast_in_dim.13, s32[1024]{0:T(1024)S(1)} %broadcast_clamp_fusion.3), kind=kCustom, calls=%fused_computation | custom fusion | bytes 20480 | tf_op jit(solution)/shard_map/gather | solution.py:115
  49.7 4.0 %collective-permute-start.6 = (f32[2,20,4,1]{3,2,1,0:T(4,128)S(1)}, f32[2,20,4,1]{3,2,1,0:T(4,128)S(1)}, u32[]{:S(2)}, u32[]{:S(2)}) collective-permute-start(f32[2,20,4,1]{3,2,1,0:T(4,128)S(1)} %get-tuple-element.158), channel_id=1, source_target_pairs={{0,1},{1,2},{2,3},{3,4},{4,5},{5,6},{6,7},{7,8},{8,9},{9,10},{10,1... | collective-permute-start | bytes 1928 | tf_op jit(solution)/shard_map/ppermute | solution.py:24
  53.7 1.3 collective-permute-start.7
  55.2 0.7 dynamic-slice
  55.8 5.7 %collective-permute-done.7 = f32[2,20,4,1]{3,2,1,0:T(4,128)S(1)} collective-permute-done((f32[2,20,4,1]{3,2,1,0:T(4,128)S(1)}, f32[2,20,4,1]{3,2,1,0:T(4,128)S(1)}, u32[]{:S(2)}, u32[]{:S(2)}) %collective-permute-start.7) | collective-permute-done | bytes 672 | tf_op jit(solution)/shard_map/ppermute | solution.py:26
  61.5 0.4 pad_maximum_fusion.4
  62.1 0.2 multiply_multiply_fusion.1
  62.9 1.2 fusion.113
  64.3 1.4 scatter_custom_fusion
  65.8 29.6 %all-gather = f32[16,64,2]{1,2,0:T(2,128)S(1)} all-gather(f32[1,64,2]{1,2,0:T(2,128)S(1)} %bitcast.468), channel_id=1, replica_groups=mesh['px'=64,'py'=16] {'py'}, dimensions={0}, use_global_device_ids=true | all-gather | bytes 8704 | tf_op jit(solution)/shard_map/all_gather | solution.py:164
  95.5 0.2 copy.33
  95.7 2.8 %gather_fusion.5 = f32[1024,2]{1,0:T(8,128)S(1)} fusion(f32[2,1024]{0,1:T(8,128)S(1)} %copy.33, s32[1024]{0:T(1024)S(1)} %get-tuple-element.274), kind=kCustom, calls=%fused_computation.5 | custom fusion | bytes 20480 | tf_op jit(solution)/shard_map/gather | solution.py:115
  98.6 2.8 %gather_fusion.6 = f32[1024,2]{1,0:T(8,128)S(1)} fusion(f32[2,1024]{0,1:T(8,128)S(1)} %copy.33, s32[1024]{0:T(1024)S(1)} %get-tuple-element.273), kind=kCustom, calls=%fused_computation.6 | custom fusion | bytes 20480 | tf_op jit(solution)/shard_map/gather | solution.py:115
  101.4 2.8 %gather_fusion.4 = f32[1024,2]{1,0:T(8,128)S(1)} fusion(f32[2,1024]{0,1:T(8,128)S(1)} %copy.33, s32[1024]{0:T(1024)S(1)} %broadcast_clamp_fusion.3), kind=kCustom, calls=%fused_computation.4 | custom fusion | bytes 20480 | tf_op jit(solution)/shard_map/gather | solution.py:115
  104.2 2.8 %gather_fusion.7 = f32[1024,2]{1,0:T(8,128)S(1)} fusion(f32[2,1024]{0,1:T(8,128)S(1)} %copy.33, s32[1024]{0:T(1024)S(1)} %get-tuple-element.272), kind=kCustom, calls=%fused_computation.7 | custom fusion | bytes 20480 | tf_op jit(solution)/shard_map/gather | solution.py:115
  107.2 0.2 copy.38
  107.4 0.2 copy.34
  107.8 0.2 copy.41
  108.1 2.8 %gather_fusion.9 = f32[1024,2]{1,0:T(8,128)S(1)} fusion(f32[2,1024]{0,1:T(8,128)S(1)} %copy.41, s32[1024]{0:T(1024)S(1)} %get-tuple-element.274), kind=kCustom, calls=%fused_computation.9 | custom fusion | bytes 20480 | tf_op jit(solution)/shard_map/gather | solution.py:115
  110.9 2.8 %gather_fusion.10 = f32[1024,2]{1,0:T(8,128)S(1)} fusion(f32[2,1024]{0,1:T(8,128)S(1)} %copy.41, s32[1024]{0:T(1024)S(1)} %get-tuple-element.273), kind=kCustom, calls=%fused_computation.10 | custom fusion | bytes 20480 | tf_op jit(solution)/shard_map/gather | solution.py:115
  113.7 2.8 %gather_fusion.8 = f32[1024,2]{1,0:T(8,128)S(1)} fusion(f32[2,1024]{0,1:T(8,128)S(1)} %copy.41, s32[1024]{0:T(1024)S(1)} %broadcast_clamp_fusion.3), kind=kCustom, calls=%fused_computation.8 | custom fusion | bytes 20480 | tf_op jit(solution)/shard_map/gather | solution.py:115
  116.5 2.8 %gather_fusion.11 = f32[1024,2]{1,0:T(8,128)S(1)} fusion(f32[2,1024]{0,1:T(8,128)S(1)} %copy.41, s32[1024]{0:T(1024)S(1)} %get-tuple-element.272), kind=kCustom, calls=%fused_computation.11 | custom fusion | bytes 20480 | tf_op jit(solution)/shard_map/gather | solution.py:115
  120.2 0.2 copy.49
  120.4 2.8 %gather_fusion.12 = f32[1024,2]{1,0:T(8,128)S(1)} fusion(f32[2,1024]{0,1:T(8,128)S(1)} %copy.49, s32[1024]{0:T(1024)S(1)} %broadcast_clamp_fusion.3), kind=kCustom, calls=%fused_computation.12 | custom fusion | bytes 20480 | tf_op jit(solution)/shard_map/gather | solution.py:115
  123.2 2.8 %gather_fusion.13 = f32[1024,2]{1,0:T(8,128)S(1)} fusion(f32[2,1024]{0,1:T(8,128)S(1)} %copy.49, s32[1024]{0:T(1024)S(1)} %get-tuple-element.274), kind=kCustom, calls=%fused_computation.13 | custom fusion | bytes 20480 | tf_op jit(solution)/shard_map/gather | solution.py:115
  126.0 2.8 %gather_fusion.14 = f32[1024,2]{1,0:T(8,128)S(1)} fusion(f32[2,1024]{0,1:T(8,128)S(1)} %copy.49, s32[1024]{0:T(1024)S(1)} %get-tuple-element.273), kind=kCustom, calls=%fused_computation.14 | custom fusion | bytes 20480 | tf_op jit(solution)/shard_map/gather | solution.py:115
  128.8 2.8 %gather_fusion.15 = f32[1024,2]{1,0:T(8,128)S(1)} fusion(f32[2,1024]{0,1:T(8,128)S(1)} %copy.49, s32[1024]{0:T(1024)S(1)} %get-tuple-element.272), kind=kCustom, calls=%fused_computation.15 | custom fusion | bytes 20480 | tf_op jit(solution)/shard_map/gather | solution.py:115
  132.5 0.7 copy-done.50
  133.3 0.9 gather_fusion.16
  134.3 14.5 %collective-permute-start.8 = (f32[2,20,1,128]{3,2,1,0:T(1,128)S(1)}, f32[2,20,1,128]{3,2,1,0:T(1,128)S(1)}, u32[]{:S(2)}, u32[]{:S(2)}) collective-permute-start(f32[2,20,1,128]{3,2,1,0:T(1,128)S(1)} %get-tuple-element.170), channel_id=1, source_target_pairs={{0,16},{16,32},{32,48},{48,64},{64,80},{80,96},{96,112},{112,128},... | collective-permute-start | bytes 61448 | tf_op jit(solution)/shard_map/ppermute | solution.py:24
  148.9 1.9 %collective-permute-start.9 = (f32[2,20,1,128]{3,2,1,0:T(1,128)S(1)}, f32[2,20,1,128]{3,2,1,0:T(1,128)S(1)}, u32[]{:S(2)}, u32[]{:S(2)}) collective-permute-start(f32[2,20,1,128]{3,2,1,0:T(1,128)S(1)} %get-tuple-element.171), channel_id=1, source_target_pairs={{16,0},{32,16},{48,32},{64,48},{80,64},{96,80},{112,96},{128,112},... | collective-permute-start | bytes 61448 | tf_op jit(solution)/shard_map/ppermute | solution.py:26
  150.8 6.5 %collective-permute-done.9 = f32[2,20,1,128]{3,2,1,0:T(1,128)S(1)} collective-permute-done((f32[2,20,1,128]{3,2,1,0:T(1,128)S(1)}, f32[2,20,1,128]{3,2,1,0:T(1,128)S(1)}, u32[]{:S(2)}, u32[]{:S(2)}) %collective-permute-start.9) | collective-permute-done | bytes 20512 | tf_op jit(solution)/shard_map/ppermute | solution.py:26
  157.5 1.3 collective-permute-start.10
  158.8 1.3 collective-permute-start.11
  160.3 3.7 %collective-permute-done.11 = f32[2,20,4,1]{3,2,1,0:T(4,128)S(1)} collective-permute-done((f32[2,20,4,1]{3,2,1,0:T(4,128)S(1)}, f32[2,20,4,1]{3,2,1,0:T(4,128)S(1)}, u32[]{:S(2)}, u32[]{:S(2)}) %collective-permute-start.11) | collective-permute-done | bytes 672 | tf_op jit(solution)/shard_map/ppermute | solution.py:26
  164.0 0.4 pad_maximum_fusion.6
  164.6 0.2 multiply_multiply_fusion
  165.6 1.2 fusion.35
  167.1 0.6 copy-done.29
  168.0 0.6 fusion.375
  (215 shorter events, 7.8 us)
Async XLA Ops:
  0.6 0.7 copy-start.7
  2.1 6.9 %copy-start.48 = (s32[4,2,128]{2,1,0:T(2,128)S(1)}, s32[4,2,128]{2,1,0:T(2,128)}, u32[]{:S(2)}) copy-start(s32[4,2,128]{2,1,0:T(2,128)} %param.15) | copy-start | bytes 12292
  2.2 6.9 %copy-start.5 = (s32[4,1024]{1,0:T(4,128)S(1)}, s32[4,1024]{1,0:T(4,128)}, u32[]{:S(2)}) copy-start(s32[4,1024]{1,0:T(4,128)} %param.19) | copy-start | bytes 49156
  2.2 8.2 %collective-permute-start = (f32[81,1,128]{2,1,0:T(1,128)S(1)}, f32[81,1,128]{2,1,0:T(1,128)S(1)}, u32[]{:S(2)}, u32[]{:S(2)}) collective-permute-start(f32[81,1,128]{2,1,0:T(1,128)S(1)} %get-tuple-element.138), channel_id=1, source_target_pairs={{0,16},{16,32},{32,48},{48,64},{64,80},{80,96},{96,112},{112,128},... | collective-permute-start | bytes 124424 | tf_op jit(solution)/shard_map/ppermute | solution.py:24
  7.1 8.6 %collective-permute-start.1 = (f32[81,1,128]{2,1,0:T(1,128)S(1)}, f32[81,1,128]{2,1,0:T(1,128)S(1)}, u32[]{:S(2)}, u32[]{:S(2)}) collective-permute-start(f32[81,1,128]{2,1,0:T(1,128)S(1)} %get-tuple-element.139), channel_id=1, source_target_pairs={{16,0},{32,16},{48,32},{64,48},{80,64},{96,80},{112,96},{128,112},... | collective-permute-start | bytes 124424 | tf_op jit(solution)/shard_map/ppermute | solution.py:26
  9.1 0.7 copy-start.49
  9.1 0.7 copy-start.6
  9.2 6.6 %copy-start.1 = (f32[2,20,2,128]{3,2,1,0:T(2,128)S(1)}, f32[2,20,2,128]{3,2,1,0:T(2,128)}, u32[]{:S(2)}) copy-start(f32[2,20,2,128]{3,2,1,0:T(2,128)} %param.10) | copy-start | bytes 122884
  9.8 6.0 %copy-start = (f32[2,20,2,128]{3,2,1,0:T(2,128)S(1)}, f32[2,20,2,128]{3,2,1,0:T(2,128)}, u32[]{:S(2)}) copy-start(f32[2,20,2,128]{3,2,1,0:T(2,128)} %param.11) | copy-start | bytes 122884
  16.1 6.3 %collective-permute-start.2 = (f32[81,4,1]{2,1,0:T(4,128)S(1)}, f32[81,4,1]{2,1,0:T(4,128)S(1)}, u32[]{:S(2)}, u32[]{:S(2)}) collective-permute-start(f32[81,4,1]{2,1,0:T(4,128)S(1)} %get-tuple-element.122), channel_id=1, source_target_pairs={{0,1},{1,2},{2,3},{3,4},{4,5},{5,6},{6,7},{7,8},{8,9},{9,10},{10,1... | collective-permute-start | bytes 3896 | tf_op jit(solution)/shard_map/ppermute | solution.py:24
  20.1 6.7 %collective-permute-start.3 = (f32[81,4,1]{2,1,0:T(4,128)S(1)}, f32[81,4,1]{2,1,0:T(4,128)S(1)}, u32[]{:S(2)}, u32[]{:S(2)}) collective-permute-start(f32[81,4,1]{2,1,0:T(4,128)S(1)} %get-tuple-element.123), channel_id=1, source_target_pairs={{1,0},{2,1},{3,2},{4,3},{5,4},{6,5},{7,6},{8,7},{9,8},{10,9},{11,1... | collective-permute-start | bytes 3896 | tf_op jit(solution)/shard_map/ppermute | solution.py:26
  28.7 0.7 copy-start.4
  29.5 2.4 %copy-start.8 = (f32[2,128]{1,0:T(2,128)}, f32[2,128]{1,0:T(2,128)S(1)}, u32[]{:S(2)}) copy-start(f32[2,128]{1,0:T(2,128)S(1)} %get-tuple-element.181) | copy-start | bytes 3076
  29.5 2.4 %copy-start.10 = (f32[2,128]{1,0:T(2,128)}, f32[2,128]{1,0:T(2,128)S(1)}, u32[]{:S(2)}) copy-start(f32[2,128]{1,0:T(2,128)S(1)} %get-tuple-element.182) | copy-start | bytes 3076
  29.5 2.4 %copy-start.12 = (f32[2,128]{1,0:T(2,128)}, f32[2,128]{1,0:T(2,128)S(1)}, u32[]{:S(2)}) copy-start(f32[2,128]{1,0:T(2,128)S(1)} %get-tuple-element.183) | copy-start | bytes 3076
  29.5 2.4 %copy-start.14 = (f32[2,128]{1,0:T(2,128)}, f32[2,128]{1,0:T(2,128)S(1)}, u32[]{:S(2)}) copy-start(f32[2,128]{1,0:T(2,128)S(1)} %get-tuple-element.185) | copy-start | bytes 3076
  29.5 2.3 %copy-start.16 = (f32[2,128]{1,0:T(2,128)}, f32[2,128]{1,0:T(2,128)S(1)}, u32[]{:S(2)}) copy-start(f32[2,128]{1,0:T(2,128)S(1)} %get-tuple-element.186) | copy-start | bytes 3076
  29.5 2.3 %copy-start.18 = (f32[2,128]{1,0:T(2,128)}, f32[2,128]{1,0:T(2,128)S(1)}, u32[]{:S(2)}) copy-start(f32[2,128]{1,0:T(2,128)S(1)} %get-tuple-element.187) | copy-start | bytes 3076
  29.5 2.3 %copy-start.20 = (f32[2,128]{1,0:T(2,128)}, f32[2,128]{1,0:T(2,128)S(1)}, u32[]{:S(2)}) copy-start(f32[2,128]{1,0:T(2,128)S(1)} %get-tuple-element.188) | copy-start | bytes 3076
  29.5 2.3 %copy-start.22 = (f32[2,128]{1,0:T(2,128)}, f32[2,128]{1,0:T(2,128)S(1)}, u32[]{:S(2)}) copy-start(f32[2,128]{1,0:T(2,128)S(1)} %get-tuple-element.189) | copy-start | bytes 3076
  29.5 2.3 %copy-start.24 = (f32[2,128]{1,0:T(2,128)}, f32[2,128]{1,0:T(2,128)S(1)}, u32[]{:S(2)}) copy-start(f32[2,128]{1,0:T(2,128)S(1)} %get-tuple-element.190) | copy-start | bytes 3076
  29.6 2.3 %copy-start.26 = (f32[2,128]{1,0:T(2,128)}, f32[2,128]{1,0:T(2,128)S(1)}, u32[]{:S(2)}) copy-start(f32[2,128]{1,0:T(2,128)S(1)} %get-tuple-element.191) | copy-start | bytes 3076
  29.8 2.3 %copy-start.28 = (f32[2,128]{1,0:T(2,128)}, f32[2,128]{1,0:T(2,128)S(1)}, u32[]{:S(2)}) copy-start(f32[2,128]{1,0:T(2,128)S(1)} %get-tuple-element.54) | copy-start | bytes 3076
  29.8 2.3 %copy-start.30 = (f32[2,128]{1,0:T(2,128)}, f32[2,128]{1,0:T(2,128)S(1)}, u32[]{:S(2)}) copy-start(f32[2,128]{1,0:T(2,128)S(1)} %get-tuple-element.58) | copy-start | bytes 3076
  29.8 2.3 %copy-start.32 = (f32[2,128]{1,0:T(2,128)}, f32[2,128]{1,0:T(2,128)S(1)}, u32[]{:S(2)}) copy-start(f32[2,128]{1,0:T(2,128)S(1)} %get-tuple-element.62) | copy-start | bytes 3076
  29.8 2.3 %copy-start.34 = (f32[2,128]{1,0:T(2,128)}, f32[2,128]{1,0:T(2,128)S(1)}, u32[]{:S(2)}) copy-start(f32[2,128]{1,0:T(2,128)S(1)} %get-tuple-element.66) | copy-start | bytes 3076
  29.8 2.3 %copy-start.36 = (f32[2,128]{1,0:T(2,128)}, f32[2,128]{1,0:T(2,128)S(1)}, u32[]{:S(2)}) copy-start(f32[2,128]{1,0:T(2,128)S(1)} %get-tuple-element.70) | copy-start | bytes 3076
  29.8 2.3 %copy-start.38 = (f32[2,128]{1,0:T(2,128)}, f32[2,128]{1,0:T(2,128)S(1)}, u32[]{:S(2)}) copy-start(f32[2,128]{1,0:T(2,128)S(1)} %get-tuple-element.74) | copy-start | bytes 3076
  29.8 2.3 %copy-start.40 = (f32[2,128]{1,0:T(2,128)}, f32[2,128]{1,0:T(2,128)S(1)}, u32[]{:S(2)}) copy-start(f32[2,128]{1,0:T(2,128)S(1)} %get-tuple-element.78) | copy-start | bytes 3076
  29.8 2.3 %copy-start.42 = (f32[2,128]{1,0:T(2,128)}, f32[2,128]{1,0:T(2,128)S(1)}, u32[]{:S(2)}) copy-start(f32[2,128]{1,0:T(2,128)S(1)} %get-tuple-element.82) | copy-start | bytes 3076
  29.8 2.3 %copy-start.44 = (f32[2,128]{1,0:T(2,128)}, f32[2,128]{1,0:T(2,128)S(1)}, u32[]{:S(2)}) copy-start(f32[2,128]{1,0:T(2,128)S(1)} %get-tuple-element.86) | copy-start | bytes 3076
  29.9 2.3 %copy-start.46 = (f32[2,128]{1,0:T(2,128)}, f32[2,128]{1,0:T(2,128)S(1)}, u32[]{:S(2)}) copy-start(f32[2,128]{1,0:T(2,128)S(1)} %get-tuple-element.88) | copy-start | bytes 3076
  29.9 0.8 copy-start.3
  32.5 5.0 %copy-start.2 = (f32[1024]{0:T(1024)S(1)}, f32[1024]{0:T(1024)}, u32[]{:S(2)}) copy-start(f32[1024]{0:T(1024)} %param.17) | copy-start | bytes 12292
  32.6 16.9 %collective-permute-start.4 = (f32[2,20,1,128]{3,2,1,0:T(1,128)S(1)}, f32[2,20,1,128]{3,2,1,0:T(1,128)S(1)}, u32[]{:S(2)}, u32[]{:S(2)}) collective-permute-start(f32[2,20,1,128]{3,2,1,0:T(1,128)S(1)} %get-tuple-element.172), channel_id=1, source_target_pairs={{0,16},{16,32},{32,48},{48,64},{64,80},{80,96},{96,112},{112,128},... | collective-permute-start | bytes 61448 | tf_op jit(solution)/shard_map/ppermute | solution.py:24
  35.6 13.9 %collective-permute-start.5 = (f32[2,20,1,128]{3,2,1,0:T(1,128)S(1)}, f32[2,20,1,128]{3,2,1,0:T(1,128)S(1)}, u32[]{:S(2)}, u32[]{:S(2)}) collective-permute-start(f32[2,20,1,128]{3,2,1,0:T(1,128)S(1)} %get-tuple-element.173), channel_id=1, source_target_pairs={{16,0},{32,16},{48,32},{64,48},{80,64},{96,80},{112,96},{128,112},... | collective-permute-start | bytes 61448 | tf_op jit(solution)/shard_map/ppermute | solution.py:26
  49.7 6.2 %collective-permute-start.6 = (f32[2,20,4,1]{3,2,1,0:T(4,128)S(1)}, f32[2,20,4,1]{3,2,1,0:T(4,128)S(1)}, u32[]{:S(2)}, u32[]{:S(2)}) collective-permute-start(f32[2,20,4,1]{3,2,1,0:T(4,128)S(1)} %get-tuple-element.158), channel_id=1, source_target_pairs={{0,1},{1,2},{2,3},{3,4},{4,5},{5,6},{6,7},{7,8},{8,9},{9,10},{10,1... | collective-permute-start | bytes 1928 | tf_op jit(solution)/shard_map/ppermute | solution.py:24
  53.7 7.9 %collective-permute-start.7 = (f32[2,20,4,1]{3,2,1,0:T(4,128)S(1)}, f32[2,20,4,1]{3,2,1,0:T(4,128)S(1)}, u32[]{:S(2)}, u32[]{:S(2)}) collective-permute-start(f32[2,20,4,1]{3,2,1,0:T(4,128)S(1)} %get-tuple-element.159), channel_id=1, source_target_pairs={{1,0},{2,1},{3,2},{4,3},{5,4},{6,5},{7,6},{8,7},{9,8},{10,9},{11,1... | collective-permute-start | bytes 1928 | tf_op jit(solution)/shard_map/ppermute | solution.py:26
  132.5 0.7 copy-start.50
  134.3 16.5 %collective-permute-start.8 = (f32[2,20,1,128]{3,2,1,0:T(1,128)S(1)}, f32[2,20,1,128]{3,2,1,0:T(1,128)S(1)}, u32[]{:S(2)}, u32[]{:S(2)}) collective-permute-start(f32[2,20,1,128]{3,2,1,0:T(1,128)S(1)} %get-tuple-element.170), channel_id=1, source_target_pairs={{0,16},{16,32},{32,48},{48,64},{64,80},{80,96},{96,112},{112,128},... | collective-permute-start | bytes 61448 | tf_op jit(solution)/shard_map/ppermute | solution.py:24
  148.9 8.4 %collective-permute-start.9 = (f32[2,20,1,128]{3,2,1,0:T(1,128)S(1)}, f32[2,20,1,128]{3,2,1,0:T(1,128)S(1)}, u32[]{:S(2)}, u32[]{:S(2)}) collective-permute-start(f32[2,20,1,128]{3,2,1,0:T(1,128)S(1)} %get-tuple-element.171), channel_id=1, source_target_pairs={{16,0},{32,16},{48,32},{64,48},{80,64},{96,80},{112,96},{128,112},... | collective-permute-start | bytes 61448 | tf_op jit(solution)/shard_map/ppermute | solution.py:26
  157.5 2.8 %collective-permute-start.10 = (f32[2,20,4,1]{3,2,1,0:T(4,128)S(1)}, f32[2,20,4,1]{3,2,1,0:T(4,128)S(1)}, u32[]{:S(2)}, u32[]{:S(2)}) collective-permute-start(f32[2,20,4,1]{3,2,1,0:T(4,128)S(1)} %get-tuple-element.148), channel_id=1, source_target_pairs={{0,1},{1,2},{2,3},{3,4},{4,5},{5,6},{6,7},{7,8},{8,9},{9,10},{10,1... | collective-permute-start | bytes 1928 | tf_op jit(solution)/shard_map/ppermute | solution.py:24
  158.8 5.2 %collective-permute-start.11 = (f32[2,20,4,1]{3,2,1,0:T(4,128)S(1)}, f32[2,20,4,1]{3,2,1,0:T(4,128)S(1)}, u32[]{:S(2)}, u32[]{:S(2)}) collective-permute-start(f32[2,20,4,1]{3,2,1,0:T(4,128)S(1)} %get-tuple-element.149), channel_id=1, source_target_pairs={{1,0},{2,1},{3,2},{4,3},{5,4},{6,5},{7,6},{8,7},{9,8},{10,9},{11,1... | collective-permute-start | bytes 1928 | tf_op jit(solution)/shard_map/ppermute | solution.py:26
  165.4 1.4 copy-start.9
  165.4 1.4 copy-start.11
  165.4 1.4 copy-start.13
  165.4 1.4 copy-start.15
  165.4 1.4 copy-start.17
  165.4 1.4 copy-start.19
  165.4 1.4 copy-start.21
  165.4 1.4 copy-start.23
  165.4 1.4 copy-start.25
  165.5 1.4 copy-start.27
  165.5 1.5 copy-start.31
  165.5 1.5 copy-start.33
  165.5 1.5 copy-start.35
  165.5 1.5 copy-start.37
  165.5 1.5 copy-start.39
  165.5 1.5 copy-start.41
  165.5 1.5 copy-start.43
  165.5 1.5 copy-start.45
  165.5 1.5 copy-start.47
  167.0 0.7 copy-start.29
where the time goes:
time: 169 us
  local copies, waits for them, and re-layouts  55.5 us (33%)
  starting transfers between devices  41.5 us (25%)
  blocking collectives  29.6 us (18%)
  waiting for transfers between devices  26.8 us (16%)
  other arithmetic  13.1 us (8%)
  between operations  2.14 us (1%)
    gather x32, local copies, waits for them, and re-layouts, jacobi_sweep(): applied = applied + vals[slot] * whole[:, cols[slot]]  48 us
    ppermute x6, starting transfers between devices, extended_2(): lax.ppermute(tail, axis, [(i, (i + 1) % count) for i in range(ends)])  31.8 us
    all_gather x1, blocking collectives, body(): whole = lax.all_gather(restricted, 'py', axis=1, tiled=True)  29.6 us
    ppermute x6, waiting for transfers between devices, extended_2(): lax.ppermute(head, axis, [((i + 1) % count, i) for i in range(ends)])  25.7 us
    ppermute x6, starting transfers between devices, extended_2(): lax.ppermute(head, axis, [((i + 1) % count, i) for i in range(ends)])  9.64 us
    unnamed x129, local copies, waits for them, and re-layouts  4.16 us
  transfers between devices with their start and end apart: 12, of which 7 were waited for; matrix products, arithmetic and copies ran while one was open for 8% of the time, Pallas kernels for 0%

commit v1 on v0

v1 whole, which is shorter than its diff:
```python
import functools

import jax
import jax.numpy as jnp
from jax import lax
from jax.experimental import pallas as pl
from jax.experimental.pallas import tpu as pltpu
from jax.sharding import PartitionSpec as P

CITERS = 4
AGG_DEV = 64
KZ = 4.0
EPS0 = 0.05
OMEGA = 0.8
OFFSETS = ((-1, -1), (-1, 0), (-1, 1), (0, -1), (0, 1), (1, -1), (1, 0), (1, 1))
MESH = pl.DeviceIdType.MESH
LAYERS = 20
F32 = jnp.float32
I32 = jnp.int32

FIELD = 64


def turn(x, shift, axis):
    shift %= x.shape[axis]
    return pltpu.roll(x, shift, axis) if shift else x


def stacked(tiles):
    return jnp.concatenate([t[None] for t in tiles], axis=0)


def vertical(x):
    return jnp.concatenate([x[1:], x[-1:]], axis=0) - jnp.concatenate([x[:1], x[:-1]], axis=0)


def kernel(
    n_px,
    n_py,
    velocity,
    direction,
    forcing,
    softness,
    friction,
    links,
    aggregate,
    coarse_diag,
    coarse_vals,
    coarse_cols,
    image_out,
    answer_out,
    vx,
    vx_recv,
    fo,
    fr,
    lk,
    ag,
    dg,
    cv,
    cc,
    edge_send,
    edge_recv,
    sm,
    sm_recv,
    edge2_send,
    edge2_recv,
    rs,
    rr,
    xs,
    ct,
    cr,
    cs,
    ds_,
    ws,
    img,
    ans,
    load_sem,
    send_sem,
    recv_sem,
    out_sem,
):
    px = lax.axis_index("px")
    py = lax.axis_index("py")
    n_hi = n_py // 2

    def wrap(value, count):
        return lax.rem(value + count, count)

    def peer(dx, dy):
        return (wrap(px + dx, n_px), wrap(py + dy, n_py))

    loads = []

    def load(src, dst):
        copy = pltpu.make_async_copy(src, dst, load_sem.at[len(loads)])
        copy.start()
        loads.append(copy)

    for c in range(2):
        own = pl.ds(4 * c + 1, 2)
        load(velocity.at[c], vx.at[pl.ds(0, LAYERS), own])
        load(direction.at[c], vx.at[pl.ds(LAYERS, LAYERS), own])
        load(softness, vx.at[2 * LAYERS, own])
        load(aggregate, ag.at[own])
    first_loads = len(loads)

    sides = [(dx, dy) for dx in (-1, 0, 1) for dy in (-1, 0, 1) if (dx, dy) != (0, 0)]
    peers = [peer(dx, dy) for dx, dy in sides if dx != 0] + [peer(0, k) for k in range(1, n_py)]
    barrier = pltpu.get_barrier_semaphore()
    for target in peers:
        pl.semaphore_signal(barrier, inc=1, device_id=target, device_id_type=MESH)

    for c in range(2):
        own = pl.ds(4 * c + 1, 2)
        load(forcing.at[c], fo.at[:, own])
        load(friction, fr.at[own])
        load(links, lk.at[:, own])
    load(coarse_diag, dg)
    for k in range(4):
        load(coarse_vals.at[:, k], cv.at[k])
        load(coarse_cols.at[:, k], cc.at[k])

    lane = lax.broadcasted_iota(I32, (8, 128), 1)
    sub = lax.broadcasted_iota(I32, (8, 128), 0)
    row = sub & 3
    core = (row == 1) | (row == 2)
    none = 9
    row_ok = (row != jnp.where(px > 0, none, 0)) & (row != jnp.where(px < n_px - 1, none, 3))
    even = (lane & 1) == 0
    no_left = jnp.where(py > 0, none, 0)
    no_right = jnp.where(py < n_py - 1, none, 1)
    edge_ok = row_ok & ((lane & 1) != no_left) & ((lane & 1) != no_right)

    def packed(fields):
        tile = jnp.zeros((8, 128), F32)
        for x, at in fields:
            tile = jnp.where((lane >> 1) == at // 2, turn(x, at + 1, 1), tile)
        return tile

    count = [0]

    def send(src, dst, target):
        i = count[0]
        count[0] += 1
        copy = pltpu.make_async_remote_copy(
            src_ref=src,
            dst_ref=dst,
            send_sem=send_sem.at[i],
            recv_sem=recv_sem.at[i],
            device_id=target,
            device_id_type=MESH,
        )
        copy.start()
        return copy

    def exchange_rim(src, dst, tile, tiles):
        copies = []
        for i, (dx, dy) in enumerate((dx, dy) for dy in (-1, 1) for dx in (-1, 0, 1)):
            copies.append(send(tile, tiles.at[5 - i], peer(dx, dy)))
        for c in range(2):
            copies.append(
                send(src.at[:, pl.ds(4 * c + 2, 1)], dst.at[:, pl.ds(4 * c, 1)], peer(1, 0))
            )
            copies.append(
                send(src.at[:, pl.ds(4 * c + 1, 1)], dst.at[:, pl.ds(4 * c + 3, 1)], peer(-1, 0))
            )
        return copies

    def edges_of(tiles):
        def column(first):
            below, here, above = tiles[first], tiles[first + 1], tiles[first + 2]
            return jnp.where(
                row == 0, turn(below, -2, 0), jnp.where(row == 3, turn(above, 2, 0), here)
            )

        left, right = column(0), column(3)
        return jnp.where(edge_ok, jnp.where(even, left, turn(right, -2, 1)), 0.0)

    def unpacked(tile, at):
        return stacked([turn(tile, -(at + 2 * layer), 1) for layer in range(LAYERS)])

    def beside(x, ends):
        left = jnp.where(lane == 0, ends, turn(x, 1, x.ndim - 1))
        right = jnp.where(lane == 127, ends, turn(x, -1, x.ndim - 1))
        return left, x, right

    for copy in loads[:first_loads]:
        copy.wait()
    agg_own = jnp.where(core, ag[...], 0)
    edge_send[...] = packed(
        [(vx[layer], 2 * layer) for layer in range(LAYERS)]
        + [(vx[2 * LAYERS], 2 * LAYERS), (agg_own.astype(F32), 2 * LAYERS + 2)]
        + [(vx[LAYERS + layer], FIELD + 2 * layer) for layer in range(LAYERS)]
    )
    pl.semaphore_wait(barrier, len(peers))
    round1 = exchange_rim(vx, vx_recv, edge_send, edge_recv)

    for copy in loads[first_loads:]:
        copy.wait()
    rub = jnp.where(core, fr[...], 1.0)
    slots = jnp.where(core, lk[...], 8)
    halves = []
    for d, (dx, _) in enumerate(OFFSETS):
        tally = jnp.sum((slots == d).astype(F32), axis=0)
        halves.append(turn(0.5 * tally, dx, 0))
    scale = OMEGA / dg[...]
    weights = [cv[k] * scale for k in range(4)]
    cols = [cc[k] for k in range(4)]
    col_hi = [c >> 7 for c in cols]
    col_lo = [c & 127 for c in cols]

    for copy in round1:
        copy.wait_recv()

    def joined(own, rim):
        return jnp.where(row_ok, jnp.where(core, own, rim), 0.0)

    v = joined(vx[0:LAYERS], vx_recv[0:LAYERS])
    rate = joined(vx[2 * LAYERS], vx_recv[2 * LAYERS])
    edge = edges_of(edge_recv)
    top = (lane == 38) | (lane == 37) | (lane == 102) | (lane == 101)
    bottom = (lane == 0) | (lane == 127) | (lane == 64) | (lane == 63)

    def edge_vertical(tile):
        return jnp.where(top, tile, turn(tile, -2, 1)) - jnp.where(bottom, tile, turn(tile, 2, 1))

    def viscosity(shear, soft, axis):
        square = shear * shear
        strain = EPS0 + 0.25 * KZ * (square + turn(square, 4, axis))
        eta = soft * jnp.exp(jnp.log(strain) * (-1.0 / 3.0))
        slope = (-2.0 / 3.0 * 0.25 * KZ) * eta / strain * shear
        return eta, slope

    eta, slope = viscosity(vertical(v), rate, 1)
    edge_shear = edge_vertical(edge)
    edge_rate = jnp.where(even, edge[:, 40:41], edge[:, 39:40])
    edge_eta, edge_slope = viscosity(edge_shear, edge_rate, 0)
    edge_slope = turn(edge_slope, FIELD, 1)
    v_beside = beside(v, unpacked(edge, 0))
    eta_beside = beside(eta, unpacked(edge_eta, 0))

    side = jnp.zeros_like(v)
    pull = jnp.zeros_like(v)
    for dx in (-1, 0, 1):
        eta_here = turn(eta, dx, 1)
        v_here = turn(v, dx, 1)
        side_part = jnp.zeros_like(v)
        pull_part = jnp.zeros_like(v)
        for d, (ox, oy) in enumerate(OFFSETS):
            if ox != dx:
                continue
            couple = halves[d] * (eta_here + eta_beside[oy + 1])
            drop = halves[d] * (v_here - v_beside[oy + 1])
            cs[d] = couple
            ds_[d] = drop
            side_part = side_part + couple
            pull_part = pull_part + drop
        side = side + turn(side_part, -dx, 1)
        pull = pull + turn(pull_part, -dx, 1)
    face = (0.5 * KZ) * (eta[:-1] + eta[1:])
    jump = (0.5 * KZ) * (v[1:] - v[:-1])

    def jacobian(x, x_edge):
        rise = slope * vertical(x)
        deta = rise + turn(rise, 4, 1)
        edge_rise = edge_slope * edge_vertical(x_edge)
        edge_deta = edge_rise + turn(edge_rise, 4, 0)
        x_beside = beside(x, unpacked(x_edge, FIELD))
        deta_beside = beside(deta, unpacked(edge_deta, FIELD))
        total = side * x + pull * deta
        for dx in (-1, 0, 1):
            part = jnp.zeros_like(x)
            for d, (ox, oy) in enumerate(OFFSETS):
                if ox != dx:
                    continue
                part = part + (ds_[d] * deta_beside[oy + 1] - cs[d] * x_beside[oy + 1])
            total = total + turn(part, -dx, 1)
        flux = face * (x[1:] - x[:-1]) + jump * (deta[1:] + deta[:-1])
        empty = jnp.zeros_like(flux[:1])
        total = total + jnp.concatenate([rub * x[:1] - flux[:1], flux[:-1] - flux[1:], flux[-1:]])
        return total

    x = joined(vx[LAYERS : 2 * LAYERS], vx_recv[LAYERS : 2 * LAYERS])
    image = jacobian(x, edge)
    img[...] = image
    outs = []
    for c in range(2):
        copy = pltpu.make_async_copy(
            img.at[:, pl.ds(4 * c + 1, 2)], image_out.at[c], out_sem.at[c]
        )
        copy.start()
        outs.append(copy)
    resid = jnp.where(core, fo[...], 0.0) - image

    inverse, lower, upper = [], [], []
    for layer in range(LAYERS):
        pivot = side[layer]
        if layer == 0:
            pivot = pivot + rub + face[0]
        else:
            pivot = pivot + face[layer - 1] - face[layer - 1] * upper[layer - 1]
            if layer < LAYERS - 1:
                pivot = pivot + face[layer]
        inv = 1.0 / pivot
        inverse.append(inv)
        lower.append(face[layer - 1] * inv if layer else None)
        upper.append(face[layer] * inv if layer < LAYERS - 1 else None)

    def line_solve(rhs):
        forward = [rhs[0] * inverse[0]]
        for layer in range(1, LAYERS):
            forward.append(rhs[layer] * inverse[layer] + lower[layer] * forward[-1])
        back = [forward[-1]]
        for layer in range(LAYERS - 2, -1, -1):
            back.append(forward[layer] + upper[layer] * back[-1])
        return back[::-1]

    smooth = stacked(line_solve([resid[layer] for layer in range(LAYERS)]))
    sm[...] = smooth
    edge2_send[...] = packed([(smooth[layer], FIELD + 2 * layer) for layer in range(LAYERS)])

    round2 = exchange_rim(sm, sm_recv, edge2_send, edge2_recv)
    agg_rows = [agg_own[r : r + 1, :] for r in (1, 2)]
    ids = lax.broadcasted_iota(I32, (128, 128), 0) & (AGG_DEV - 1)
    hot = [(ids == a).astype(F32) for a in agg_rows]
    for copy in round2:
        copy.wait_recv()
    smooth_ext = joined(sm[...], sm_recv[...])
    after = resid - jacobian(smooth_ext, edges_of(edge2_recv))
    mean = jnp.where(core, jnp.sum(after, axis=0) / LAYERS, 0.0)

    sums = [
        lax.dot_general(
            mean, h, (((1,), (1,)), ((), ())),
            precision=lax.Precision.HIGHEST, preferred_element_type=F32,
        )
        for h in hot
    ]
    first = sums[0][1:2] + sums[1][2:3]
    second = sums[0][5:6] + sums[1][6:7]
    mine = jnp.where(lane[0:1] < AGG_DEV, first, second)
    rs[0] = mine
    place = lax.rem(py, 2) * n_hi + lax.div(py, 2)
    round3 = []
    for k in range(1, n_py):
        round3.append(send(rs, rr.at[pl.ds(place, 1)], peer(0, k)))
    rr[place] = mine

    for d, (dx, _) in enumerate(OFFSETS):
        ws[:, d] = turn(cs[d], -dx, 1)
    rest = line_solve([after[layer] for layer in range(LAYERS)])
    for layer in range(LAYERS):
        ans[layer] = smooth[layer] + rest[layer]
    held = ws[0] * inverse[0]
    ws[0] = held
    for layer in range(1, LAYERS):
        held = ws[layer] * inverse[layer] + lower[layer] * held
        ws[layer] = held
    for layer in range(LAYERS - 2, -1, -1):
        held = ws[layer] + upper[layer] * held
        ws[layer] = held

    for copy in round3:
        copy.wait_recv()
    evens, odds = rr[0:n_hi, 0, :], rr[n_hi : 2 * n_hi, 0, :]
    low = lax.broadcasted_iota(I32, (n_hi, 128), 1) < AGG_DEV
    target = [
        jnp.where(low, evens, turn(odds, AGG_DEV, 1)) * scale,
        jnp.where(low, turn(evens, AGG_DEV, 1), odds) * scale,
    ]

    def picked(source, at):
        return jnp.take_along_axis(source, at, axis=1, mode="promise_in_bounds")

    iterate = target
    for _ in range(CITERS - 1):
        later = []
        for c in range(2):
            rows = [
                jnp.broadcast_to(iterate[c][h : h + 1], (n_hi, 128)) for h in range(n_hi)
            ]
            value = (1.0 - OMEGA) * iterate[c] + target[c]
            for k in range(4):
                found = picked(rows[0], col_lo[k])
                for h in range(1, n_hi):
                    found = jnp.where(col_hi[k] == h, picked(rows[h], col_lo[k]), found)
                value = value - weights[k] * found
            later.append(value)
        iterate = later
    xs[0] = iterate[0]
    xs[1] = iterate[1]

    def corrected(owner, at):
        h = lax.div(owner, 2)
        source = jnp.where(
            sub < 4,
            jnp.broadcast_to(xs[0, pl.ds(h, 1), :], (8, 128)),
            jnp.broadcast_to(xs[1, pl.ds(h, 1), :], (8, 128)),
        )
        return picked(source, at + AGG_DEV * lax.rem(owner, 2))

    edge_agg = edge.astype(I32)
    agg_left = jnp.broadcast_to(edge_agg[:, 42:43], (8, 128))
    agg_right = jnp.broadcast_to(edge_agg[:, 41:42], (8, 128))
    corr = corrected(py, agg_own)
    corr_edge = jnp.where(
        lane < 64,
        corrected(wrap(py - 1, n_py), agg_left),
        corrected(wrap(py + 1, n_py), agg_right),
    )
    half = lane >> 6
    corr_edge = jnp.where((half != no_left) & (half != no_right), corr_edge, 0.0)
    ct[0] = corr
    ct[1] = corr_edge

    round4 = [send(ct, cr.at[0], peer(1, 0)), send(ct, cr.at[1], peer(-1, 0))]
    for copy in round4:
        copy.wait_recv()

    def rows_joined(i, own):
        joined = jnp.where(
            row == 0, turn(cr[0, i], -2, 0), jnp.where(row == 3, turn(cr[1, i], 2, 0), own)
        )
        return jnp.where(row_ok, joined, 0.0)

    corr_beside = beside(rows_joined(0, corr), rows_joined(1, corr_edge))
    result = ans[...]
    for d, (dx, dy) in enumerate(OFFSETS):
        result = result + ws[:, d] * turn(corr_beside[dy + 1], -dx, 0)
    ans[...] = result
    for c in range(2):
        copy = pltpu.make_async_copy(
            ans.at[:, pl.ds(4 * c + 1, 2)], answer_out.at[c], out_sem.at[2 + c]
        )
        copy.start()
        outs.append(copy)
    for copy in round1 + round2 + round3 + round4:
        copy.wait_send()
    for copy in outs:
        copy.wait()


def solution(mesh):
    n_px, n_py = mesh.shape["px"], mesh.shape["py"]
    n_hi = n_py // 2
    n_sends = 10 + 10 + (n_py - 1) + 2

    def body(
        velocity, direction, forcing, softness, friction, links, aggregate, diag, vals, cols
    ):
        block = jax.ShapeDtypeStruct(velocity.shape, F32)
        return pl.pallas_call(
            functools.partial(kernel, n_px, n_py),
            out_shape=(block, block),
            in_specs=[pl.BlockSpec(memory_space=pltpu.HBM)] * 10,
            out_specs=[pl.BlockSpec(memory_space=pltpu.HBM)] * 2,
            scratch_shapes=[
                pltpu.VMEM((2 * LAYERS + 1, 8, 128), F32),
                pltpu.VMEM((2 * LAYERS + 1, 8, 128), F32),
                pltpu.VMEM((LAYERS, 8, 128), F32),
                pltpu.VMEM((8, 128), F32),
                pltpu.VMEM((4, 8, 128), I32),
                pltpu.VMEM((8, 128), I32),
                pltpu.VMEM((n_hi, 128), F32),
                pltpu.VMEM((4, n_hi, 128), F32),
                pltpu.VMEM((4, n_hi, 128), I32),
                pltpu.VMEM((8, 128), F32),
                pltpu.VMEM((6, 8, 128), F32),
                pltpu.VMEM((LAYERS, 8, 128), F32),
                pltpu.VMEM((LAYERS, 8, 128), F32),
                pltpu.VMEM((8, 128), F32),
                pltpu.VMEM((6, 8, 128), F32),
                pltpu.VMEM((1, 1, 128), F32),
                pltpu.VMEM((n_py, 1, 128), F32),
                pltpu.VMEM((2, n_hi, 128), F32),
                pltpu.VMEM((2, 8, 128), F32),
                pltpu.VMEM((2, 2, 8, 128), F32),
                pltpu.VMEM((8, LAYERS, 8, 128), F32),
                pltpu.VMEM((8, LAYERS, 8, 128), F32),
                pltpu.VMEM((LAYERS, 8, 8, 128), F32),
                pltpu.VMEM((LAYERS, 8, 128), F32),
                pltpu.VMEM((LAYERS, 8, 128), F32),
                pltpu.SemaphoreType.DMA((23,)),
                pltpu.SemaphoreType.DMA((n_sends,)),
                pltpu.SemaphoreType.DMA((n_sends,)),
                pltpu.SemaphoreType.DMA((4,)),
            ],
            compiler_params=pltpu.CompilerParams(
                collective_id=0, has_side_effects=True, vmem_limit_bytes=32 * 1024 * 1024
            ),
        )(
            velocity,
            direction,
            forcing,
            softness,
            friction,
            links,
            aggregate,
            diag.reshape(n_hi, 128),
            vals.reshape(4, n_hi, 128).transpose(1, 0, 2),
            cols.reshape(4, n_hi, 128).transpose(1, 0, 2),
        )

    return jax.shard_map(
        body,
        mesh=mesh,
        in_specs=(
            P(None, None, "px", "py"),
            P(None, None, "px", "py"),
            P(None, None, "px", "py"),
            P("px", "py"),
            P("px", "py"),
            P(None, "px", "py"),
            P("px", "py"),
            P("px"),
            P(None, "px"),
            P(None, "px"),
        ),
        out_specs=(P(None, None, "px", "py"), P(None, None, "px", "py")),
        check_vma=False,
    )
```

time: 169 us -> 53.6 us (0.32)
  local copies, waits for them, and re-layouts: 55.5 us -> 7.73 us
  Pallas kernels: 0 us -> 44.7 us
  starting transfers between devices: 41.5 us -> 0 us
  blocking collectives: 29.6 us -> 0 us
  waiting for transfers between devices: 26.8 us -> 0 us
  other arithmetic: 13.1 us -> 0 us
    gather x34 -> x0, local copies, waits for them, and re-layouts: 49 us -> none  [the longest x32 48 us: jacobi_sweep(): applied = applied + vals[slot] * whole[:, cols[slot]]]
    pallas_call x0 -> x1, Pallas kernels: none -> 44.7 us  [body(): pl.pallas_call(functools.partial(kernel, n_px, n_py), out_shape=(block, b...]
    ppermute x12 -> x0, starting transfers between devices: 41.5 us -> none  [the longest x6 31.8 us: extended_2(): lax.ppermute(tail, axis, [(i, (i + 1) % count) for i in range(ends)])]
    all_gather x1 -> x0, blocking collectives: 29.6 us -> none  [body(): whole = lax.all_gather(restricted, 'py', axis=1, tiled=True)]
    ppermute x12 -> x0, waiting for transfers between devices: 26.8 us -> none  [the longest x6 25.7 us: extended_2(): lax.ppermute(head, axis, [((i + 1) % count, i) for i in range(ends)])]
    unnamed x129 -> x22, local copies, waits for them, and re-layouts: 4.16 us -> 7.73 us
    sub x3 -> x0, other arithmetic: 2.6 us -> none  [the longest x1 1.22 us: body(): final = resid - jacobian(coarse_ext)]
    concatenate x7 -> x0, other arithmetic: 2.46 us -> none  [the longest x6 1.62 us: extended_2(): jnp.concatenate([lax.ppermute(tail, axis, [(i, (i + 1) % count) for i in...]
  transfers between devices with their start and end apart: 12 -> 0, of which waited for: 7 -> 0; matrix products, arithmetic and copies ran while one was open for 8% -> 0% of each run, Pallas kernels for 0% -> 0%
where the time goes in v1:
time: 53.6 us; the launch traced here: 53.1 us
  Pallas kernels  44.7 us (83%)
  local copies, waits for them, and re-layouts  7.73 us (14%)
  between operations  0.67 us (1%)
    pallas_call x1, Pallas kernels, body(): pl.pallas_call(functools.partial(kernel, n_px, n_py), out_shape=(block, b...  44.7 us
    unnamed x22, local copies, waits for them, and re-layouts  7.73 us

profile of v1, /device:TPU:31, one launch (start us, length us, event | category | flops | bytes accessed | tf_op | source)
XLA Modules:
  0.0 53.1 jit_solution(888779906103155235)
XLA Ops:
  0.6 0.0 copy-start.5
  0.6 0.0 copy-start.7
  0.7 0.7 %copy-done.5 = s32[4,2,128]{2,1,0:T(2,128)S(1)} copy-done((s32[4,2,128]{2,1,0:T(2,128)S(1)}, s32[4,2,128]{2,1,0:T(2,128)}, u32[]{:S(2)}) %copy-start.5) | copy-done | bytes 4120
  1.3 0.0 copy-done.7
  1.3 0.0 copy-start
  1.3 0.8 %copy-done = f32[2,20,2,128]{3,2,1,0:T(2,128)S(1)} copy-done((f32[2,20,2,128]{3,2,1,0:T(2,128)S(1)}, f32[2,20,2,128]{3,2,1,0:T(2,128)}, u32[]{:S(2)}) %copy-start) | copy-done | bytes 40984
  2.1 0.0 copy-start.1
  2.1 0.8 %copy-done.1 = f32[2,20,2,128]{3,2,1,0:T(2,128)S(1)} copy-done((f32[2,20,2,128]{3,2,1,0:T(2,128)S(1)}, f32[2,20,2,128]{3,2,1,0:T(2,128)}, u32[]{:S(2)}) %copy-start.1) | copy-done | bytes 40984
  2.9 0.0 copy-start.2
  2.9 0.8 %copy-done.2 = f32[2,20,2,128]{3,2,1,0:T(2,128)S(1)} copy-done((f32[2,20,2,128]{3,2,1,0:T(2,128)S(1)}, f32[2,20,2,128]{3,2,1,0:T(2,128)}, u32[]{:S(2)}) %copy-start.2) | copy-done | bytes 40984
  3.7 0.0 copy-start.3
  3.7 0.7 %copy-done.3 = f32[4,1024]{1,0:T(4,128)S(1)} copy-done((f32[4,1024]{1,0:T(4,128)S(1)}, f32[4,1024]{1,0:T(4,128)}, u32[]{:S(2)}) %copy-start.3) | copy-done | bytes 16408
  4.4 0.0 copy-start.4
  4.4 0.7 %copy-done.4 = s32[4,1024]{1,0:T(4,128)S(1)} copy-done((s32[4,1024]{1,0:T(4,128)S(1)}, s32[4,1024]{1,0:T(4,128)}, u32[]{:S(2)}) %copy-start.4) | copy-done | bytes 16408
  5.1 0.0 copy-start.6
  5.1 0.7 %copy-done.6 = f32[1024]{0:T(1024)S(1)} copy-done((f32[1024]{0:T(1024)S(1)}, f32[1024]{0:T(1024)}, u32[]{:S(2)}) %copy-start.6) | copy-done | bytes 4120
  5.8 0.0 copy-start.8
  5.8 0.7 %copy-done.8 = f32[2,128]{1,0:T(2,128)S(1)} copy-done((f32[2,128]{1,0:T(2,128)S(1)}, f32[2,128]{1,0:T(2,128)}, u32[]{:S(2)}) %copy-start.8) | copy-done | bytes 1048
  6.5 0.0 copy-start.9
  6.5 0.7 %copy-done.9 = s32[2,128]{1,0:T(2,128)S(1)} copy-done((s32[2,128]{1,0:T(2,128)S(1)}, s32[2,128]{1,0:T(2,128)}, u32[]{:S(2)}) %copy-start.9) | copy-done | bytes 1048
  7.1 44.7 %shard_map.113 = (f32[2,20,2,128]{3,2,1,0:T(2,128)S(1)}, f32[2,20,2,128]{3,2,1,0:T(2,128)S(1)}) custom-call(f32[2,20,2,128]{3,2,1,0:T(2,128)S(1)} %copy-done, f32[2,20,2,128]{3,2,1,0:T(2,128)S(1)} %copy-done.1, f32[2,20,2,128]{3,2,1,0:T(2,128)S(1)} %copy-done.2, f32[2,128]{1,0:T(2,128)S(1)} %copy-done.7, f32[2,128]{1,0:T(2,128)S(1)} %copy-done.8, ...), custom_call_target="tpu_custom_call" | custom-call | tf_op jit(solution)/shard_map/pallas_call | solution.py:452
  51.9 0.6 %copy.14 = f32[2,20,2,128]{3,2,1,0:T(2,128)} copy(f32[2,20,2,128]{3,2,1,0:T(2,128)S(1)} %get-tuple-element.4) | data formatting | bytes 81920
  52.5 0.6 %copy.15 = f32[2,20,2,128]{3,2,1,0:T(2,128)} copy(f32[2,20,2,128]{3,2,1,0:T(2,128)S(1)} %get-tuple-element.5) | data formatting | bytes 81920
Async XLA Ops:
  0.6 0.7 %copy-start.5 = (s32[4,2,128]{2,1,0:T(2,128)S(1)}, s32[4,2,128]{2,1,0:T(2,128)}, u32[]{:S(2)}) copy-start(s32[4,2,128]{2,1,0:T(2,128)} %links.1) | copy-start | bytes 12292
  0.6 0.7 %copy-start.7 = (f32[2,128]{1,0:T(2,128)S(1)}, f32[2,128]{1,0:T(2,128)}, u32[]{:S(2)}) copy-start(f32[2,128]{1,0:T(2,128)} %softness.1) | copy-start | bytes 3076
  1.3 0.8 %copy-start = (f32[2,20,2,128]{3,2,1,0:T(2,128)S(1)}, f32[2,20,2,128]{3,2,1,0:T(2,128)}, u32[]{:S(2)}) copy-start(f32[2,20,2,128]{3,2,1,0:T(2,128)} %velocity.1) | copy-start | bytes 122884
  2.1 0.8 %copy-start.1 = (f32[2,20,2,128]{3,2,1,0:T(2,128)S(1)}, f32[2,20,2,128]{3,2,1,0:T(2,128)}, u32[]{:S(2)}) copy-start(f32[2,20,2,128]{3,2,1,0:T(2,128)} %direction.1) | copy-start | bytes 122884
  2.9 0.8 %copy-start.2 = (f32[2,20,2,128]{3,2,1,0:T(2,128)S(1)}, f32[2,20,2,128]{3,2,1,0:T(2,128)}, u32[]{:S(2)}) copy-start(f32[2,20,2,128]{3,2,1,0:T(2,128)} %forcing.1) | copy-start | bytes 122884
  3.7 0.7 %copy-start.3 = (f32[4,1024]{1,0:T(4,128)S(1)}, f32[4,1024]{1,0:T(4,128)}, u32[]{:S(2)}) copy-start(f32[4,1024]{1,0:T(4,128)} %param.18) | copy-start | bytes 49156
  4.4 0.7 %copy-start.4 = (s32[4,1024]{1,0:T(4,128)S(1)}, s32[4,1024]{1,0:T(4,128)}, u32[]{:S(2)}) copy-start(s32[4,1024]{1,0:T(4,128)} %param.19) | copy-start | bytes 49156
  5.1 0.7 %copy-start.6 = (f32[1024]{0:T(1024)S(1)}, f32[1024]{0:T(1024)}, u32[]{:S(2)}) copy-start(f32[1024]{0:T(1024)} %param.17) | copy-start | bytes 12292
  5.8 0.7 %copy-start.8 = (f32[2,128]{1,0:T(2,128)S(1)}, f32[2,128]{1,0:T(2,128)}, u32[]{:S(2)}) copy-start(f32[2,128]{1,0:T(2,128)} %friction.1) | copy-start | bytes 3076
  6.5 0.7 %copy-start.9 = (s32[2,128]{1,0:T(2,128)S(1)}, s32[2,128]{1,0:T(2,128)}, u32[]{:S(2)}) copy-start(s32[2,128]{1,0:T(2,128)} %aggregate.1) | copy-start | bytes 3076

commit v2 on v1

--- a/solution.py
+++ b/solution.py
@@ -19,6 +19,7 @@
 I32 = jnp.int32
 
 FIELD = 64
+REACH = 3
 
 
 def turn(x, shift, axis):
@@ -47,8 +48,8 @@
     coarse_diag,
     coarse_vals,
     coarse_cols,
-    image_out,
-    answer_out,
+    img,
+    ans,
     vx,
     vx_recv,
     fo,
@@ -72,12 +73,10 @@
     cs,
     ds_,
     ws,
-    img,
-    ans,
     load_sem,
     send_sem,
     recv_sem,
-    out_sem,
+    relay,
 ):
     px = lax.axis_index("px")
     py = lax.axis_index("py")
@@ -88,6 +87,25 @@
 
     def peer(dx, dy):
         return (wrap(px + dx, n_px), wrap(py + dy, n_py))
+
+    sides = [(dx, dy) for dx in (-1, 1) for dy in (-1, 1, 0)]
+    near = [k for k in range(1, n_py) if min(k, n_py - k) <= REACH]
+    peers = [peer(dx, dy) for dx, dy in sides] + [peer(0, k) for k in near]
+    barrier = pltpu.get_barrier_semaphore()
+    for target in peers:
+        pl.semaphore_signal(barrier, inc=1, device_id=target, device_id_type=MESH)
+    stages = -(-(n_py // 2) // REACH) - 1
+
+    def relay_signal(stage):
+        if stage < stages:
+            for k in (REACH, n_py - REACH):
+                pl.semaphore_signal(
+                    relay.at[stage], inc=1, device_id=peer(0, k), device_id_type=MESH
+                )
+
+    def relay_wait(stage):
+        if stage < stages:
+            pl.semaphore_wait(relay.at[stage], 2)
 
     loads = []
 
@@ -103,12 +121,6 @@
         load(softness, vx.at[2 * LAYERS, own])
         load(aggregate, ag.at[own])
     first_loads = len(loads)
-
-    sides = [(dx, dy) for dx in (-1, 0, 1) for dy in (-1, 0, 1) if (dx, dy) != (0, 0)]
-    peers = [peer(dx, dy) for dx, dy in sides if dx != 0] + [peer(0, k) for k in range(1, n_py)]
-    barrier = pltpu.get_barrier_semaphore()
-    for target in peers:
-        pl.semaphore_signal(barrier, inc=1, device_id=target, device_id_type=MESH)
 
     for c in range(2):
         own = pl.ds(4 * c + 1, 2)
@@ -154,9 +166,15 @@
         return copy
 
     def exchange_rim(src, dst, tile, tiles):
+        slot = {(dx, dy): 3 * (dy > 0) + dx + 1 for dx in (-1, 0, 1) for dy in (-1, 1)}
         copies = []
-        for i, (dx, dy) in enumerate((dx, dy) for dy in (-1, 1) for dx in (-1, 0, 1)):
-            copies.append(send(tile, tiles.at[5 - i], peer(dx, dy)))
+
+        def tile_to(dx, dy):
+            copies.append(send(tile, tiles.at[slot[-dx, -dy]], peer(dx, dy)))
+
+        for dx in (-1, 1):
+            for dy in (-1, 1):
+                tile_to(dx, dy)
         for c in range(2):
             copies.append(
                 send(src.at[:, pl.ds(4 * c + 2, 1)], dst.at[:, pl.ds(4 * c, 1)], peer(1, 0))
@@ -164,6 +182,8 @@
             copies.append(
                 send(src.at[:, pl.ds(4 * c + 1, 1)], dst.at[:, pl.ds(4 * c + 3, 1)], peer(-1, 0))
             )
+        for dy in (-1, 1):
+            tile_to(0, dy)
         return copies
 
     def edges_of(tiles):
@@ -193,6 +213,7 @@
         + [(vx[LAYERS + layer], FIELD + 2 * layer) for layer in range(LAYERS)]
     )
     pl.semaphore_wait(barrier, len(peers))
+    relay_signal(0)
     round1 = exchange_rim(vx, vx_recv, edge_send, edge_recv)
 
     for copy in loads[first_loads:]:
@@ -211,6 +232,9 @@
 
     for copy in round1:
         copy.wait_recv()
+
+    relay_wait(0)
+    relay_signal(1)
 
     def joined(own, rim):
         return jnp.where(row_ok, jnp.where(core, own, rim), 0.0)
@@ -283,13 +307,6 @@
     x = joined(vx[LAYERS : 2 * LAYERS], vx_recv[LAYERS : 2 * LAYERS])
     image = jacobian(x, edge)
     img[...] = image
-    outs = []
-    for c in range(2):
-        copy = pltpu.make_async_copy(
-            img.at[:, pl.ds(4 * c + 1, 2)], image_out.at[c], out_sem.at[c]
-        )
-        copy.start()
-        outs.append(copy)
     resid = jnp.where(core, fo[...], 0.0) - image
 
     inverse, lower, upper = [], [], []
@@ -325,6 +342,7 @@
     hot = [(ids == a).astype(F32) for a in agg_rows]
     for copy in round2:
         copy.wait_recv()
+    relay_wait(1)
     smooth_ext = joined(sm[...], sm_recv[...])
     after = resid - jacobian(smooth_ext, edges_of(edge2_recv))
     mean = jnp.where(core, jnp.sum(after, axis=0) / LAYERS, 0.0)
@@ -342,7 +360,7 @@
     rs[0] = mine
     place = lax.rem(py, 2) * n_hi + lax.div(py, 2)
     round3 = []
-    for k in range(1, n_py):
+    for k in sorted(range(1, n_py), key=lambda k: -min(k, n_py - k)):
         round3.append(send(rs, rr.at[pl.ds(place, 1)], peer(0, k)))
     rr[place] = mine
 
@@ -428,15 +446,19 @@
     for d, (dx, dy) in enumerate(OFFSETS):
         result = result + ws[:, d] * turn(corr_beside[dy + 1], -dx, 0)
     ans[...] = result
-    for c in range(2):
-        copy = pltpu.make_async_copy(
-            ans.at[:, pl.ds(4 * c + 1, 2)], answer_out.at[c], out_sem.at[2 + c]
-        )
-        copy.start()
-        outs.append(copy)
     for copy in round1 + round2 + round3 + round4:
         copy.wait_send()
-    for copy in outs:
+
+
+def write_out(image, answer, image_out, answer_out, sems):
+    copies = []
+    for c in range(2):
+        rows = pl.ds(4 * c + 1, 2)
+        copies.append(pltpu.make_async_copy(image.at[:, rows], image_out.at[c], sems.at[c]))
+        copies.append(pltpu.make_async_copy(answer.at[:, rows], answer_out.at[c], sems.at[2 + c]))
+    for copy in copies:
+        copy.start()
+    for copy in copies:
         copy.wait()
 
 
@@ -449,11 +471,12 @@
         velocity, direction, forcing, softness, friction, links, aggregate, diag, vals, cols
     ):
         block = jax.ShapeDtypeStruct(velocity.shape, F32)
-        return pl.pallas_call(
+        wide = jax.ShapeDtypeStruct((LAYERS, 8, 128), F32)
+        results = pl.pallas_call(
             functools.partial(kernel, n_px, n_py),
-            out_shape=(block, block),
+            out_shape=(wide, wide),
             in_specs=[pl.BlockSpec(memory_space=pltpu.HBM)] * 10,
-            out_specs=[pl.BlockSpec(memory_space=pltpu.HBM)] * 2,
+            out_specs=[pl.BlockSpec(memory_space=pltpu.VMEM)] * 2,
             scratch_shapes=[
                 pltpu.VMEM((2 * LAYERS + 1, 8, 128), F32),
                 pltpu.VMEM((2 * LAYERS + 1, 8, 128), F32),
@@ -478,28 +501,39 @@
                 pltpu.VMEM((8, LAYERS, 8, 128), F32),
                 pltpu.VMEM((8, LAYERS, 8, 128), F32),
                 pltpu.VMEM((LAYERS, 8, 8, 128), F32),
-                pltpu.VMEM((LAYERS, 8, 128), F32),
-                pltpu.VMEM((LAYERS, 8, 128), F32),
                 pltpu.SemaphoreType.DMA((23,)),
                 pltpu.SemaphoreType.DMA((n_sends,)),
                 pltpu.SemaphoreType.DMA((n_sends,)),
-                pltpu.SemaphoreType.DMA((4,)),
+                pltpu.SemaphoreType.REGULAR((2,)),
             ],
             compiler_params=pltpu.CompilerParams(
                 collective_id=0, has_side_effects=True, vmem_limit_bytes=32 * 1024 * 1024
             ),
         )(
-            velocity,
-            direction,
-            forcing,
-            softness,
-            friction,
-            links,
-            aggregate,
-            diag.reshape(n_hi, 128),
-            vals.reshape(4, n_hi, 128).transpose(1, 0, 2),
-            cols.reshape(4, n_hi, 128).transpose(1, 0, 2),
+            *(
+                pltpu.with_memory_space_constraint(a, pltpu.HBM)
+                for a in (
+                    velocity,
+                    direction,
+                    forcing,
+                    softness,
+                    friction,
+                    links,
+                    aggregate,
+                    diag.reshape(n_hi, 128),
+                    vals.reshape(4, n_hi, 128).transpose(1, 0, 2),
+                    cols.reshape(4, n_hi, 128).transpose(1, 0, 2),
+                )
+            )
         )
+        return pl.pallas_call(
+            write_out,
+            out_shape=(block, block),
+            in_specs=[pl.BlockSpec(memory_space=pl.ANY)] * 2,
+            out_specs=[pl.BlockSpec(memory_space=pltpu.HBM)] * 2,
+            scratch_shapes=[pltpu.SemaphoreType.DMA((4,))],
+            compiler_params=pltpu.CompilerParams(vmem_limit_bytes=8 * 1024 * 1024),
+        )(*results)
 
     return jax.shard_map(
         body,

time: 53.6 us -> 42.4 us (0.79)
  the two profiles are of different devices: /device:TPU:31 before, /device:TPU:1 now
where the time goes in v2:
time: 42.4 us; the launch traced here: 42.2 us
  Pallas kernels  41.6 us (98%)
  between operations  0.64 us (2%)
    pallas_call x1, Pallas kernels, body(): pl.pallas_call(functools.partial(kernel, n_px, n_py), out_shape=(wide, wi...  40.9 us

profile of v2, /device:TPU:1, one launch (start us, length us, event | category | flops | bytes accessed | tf_op | source)
XLA Modules:
  0.0 42.2 jit_solution(17295175854038398657)
XLA Ops:
  0.6 40.9 %shard_map.113 = (f32[20,8,128]{2,1,0:T(8,128)S(1)}, f32[20,8,128]{2,1,0:T(8,128)S(1)}) custom-call(f32[2,20,2,128]{3,2,1,0:T(2,128)} %velocity.1, f32[2,20,2,128]{3,2,1,0:T(2,128)} %direction.1, f32[2,20,2,128]{3,2,1,0:T(2,128)} %forcing.1, f32[2,128]{1,0:T(2,128)} %softness.1, f32[2,128]{1,0:T(2,128)} %friction.1, s32[4,2,128]{2,1,0:T(2,128)} %links.1, ...), custom_call_target="tpu_custom_call" | custom-call | tf_op jit(solution)/shard_map/pallas_call | solution.py:475
  41.5 0.7 %shard_map.114 = (f32[2,20,2,128]{3,2,1,0:T(2,128)}, f32[2,20,2,128]{3,2,1,0:T(2,128)}) custom-call(f32[20,8,128]{2,1,0:T(8,128)S(1)} %get-tuple-element.4.image, f32[20,8,128]{2,1,0:T(8,128)S(1)} %get-tuple-element.5.answer), custom_call_target="tpu_custom_call" | custom-call | tf_op jit(solution)/shard_map/pallas_call | solution.py:529

commit v3 on v2

v3 whole, which is shorter than its diff:
```python
import functools

import jax
import jax.numpy as jnp
from jax import lax
from jax.experimental import pallas as pl
from jax.experimental.pallas import tpu as pltpu
from jax.sharding import PartitionSpec as P

CITERS = 4
AGG_DEV = 64
KZ = 4.0
EPS0 = 0.05
OMEGA = 0.8
OFFSETS = ((-1, -1), (-1, 0), (-1, 1), (0, -1), (0, 1), (1, -1), (1, 0), (1, 1))
MESH = pl.DeviceIdType.MESH
LAYERS = 20
F32 = jnp.float32
I32 = jnp.int32

FIELD = 64
REACH = 4
V, X, RATE, LOAD, RUB, SLOT, AGG = 0, LAYERS, 2 * LAYERS, 2 * LAYERS + 1, 61, 62, 66
FAR, PLANES = 2 * LAYERS + 1, 67


def turn(x, shift, axis):
    shift %= x.shape[axis]
    return pltpu.roll(x, shift, axis) if shift else x


def stacked(tiles):
    return jnp.concatenate([t[None] for t in tiles], axis=0)


def vertical(x):
    return jnp.concatenate([x[1:], x[-1:]], axis=0) - jnp.concatenate([x[:1], x[:-1]], axis=0)


def kernel(
    n_px,
    n_py,
    velocity,
    direction,
    forcing,
    softness,
    friction,
    links,
    aggregate,
    coarse_diag,
    coarse_vals,
    coarse_cols,
    img,
    ans,
    own,
    near,
    far,
    lk,
    ag,
    dg,
    cv,
    cc,
    edge_send,
    edge_recv,
    rs,
    rr,
    xs,
    ct,
    cr,
    cs,
    ds_,
    ws,
    load_sem,
    send_sem,
    recv_sem,
    relay,
):
    px = lax.axis_index("px")
    py = lax.axis_index("py")
    n_hi = n_py // 2

    def wrap(value, count):
        return lax.rem(value + count, count)

    def peer(dx, dy):
        return (wrap(px + dx, n_px), wrap(py + dy, n_py))

    around = [peer(dx, dy) for dx in (-1, 1) for dy in (-1, 1, 0)]
    peers = around + [peer(0, k) for k in range(1, n_py) if min(k, n_py - k) <= REACH]
    barrier = pltpu.get_barrier_semaphore()
    for target in peers:
        pl.semaphore_signal(barrier, inc=1, device_id=target, device_id_type=MESH)
    relayed = n_py // 2 > REACH

    loads = []

    def load(src, dst):
        copy = pltpu.make_async_copy(src, dst, load_sem.at[len(loads)])
        copy.start()
        loads.append(copy)

    for c in range(2):
        rows = pl.ds(4 * c + 1, 2)
        load(velocity.at[c], own.at[pl.ds(V, LAYERS), rows])
        load(direction.at[c], own.at[pl.ds(X, LAYERS), rows])
        load(softness, own.at[RATE, rows])
        load(forcing.at[c], own.at[pl.ds(LOAD, LAYERS), rows])
        load(friction, own.at[RUB, rows])
        load(links, lk.at[:, rows])
        load(aggregate, ag.at[rows])
    first_loads = len(loads)
    load(coarse_diag, dg)
    for k in range(4):
        load(coarse_vals.at[:, k], cv.at[k])
        load(coarse_cols.at[:, k], cc.at[k])

    lane = lax.broadcasted_iota(I32, (8, 128), 1)
    sub = lax.broadcasted_iota(I32, (8, 128), 0)
    row = sub & 3
    core = (row == 1) | (row == 2)
    none = 9
    no_below = jnp.where(px > 0, none, 0)
    no_above = jnp.where(px < n_px - 1, none, 3)
    row_ok = (row != no_below) & (row != no_above)
    far_ok = row_ok & ((row == 0) | (row == 3))
    even = (lane & 1) == 0
    no_left = jnp.where(py > 0, none, 0)
    no_right = jnp.where(py < n_py - 1, none, 1)
    side_ok = ((lane & 1) != no_left) & ((lane & 1) != no_right)
    half = lane >> 6
    half_ok = (half != no_left) & (half != no_right)

    count = [0]

    def send(src, dst, target):
        i = count[0]
        count[0] += 1
        copy = pltpu.make_async_remote_copy(
            src_ref=src,
            dst_ref=dst,
            send_sem=send_sem.at[i],
            recv_sem=recv_sem.at[i],
            device_id=target,
            device_id_type=MESH,
        )
        copy.start()
        return copy

    def packed(fields, shift, gap):
        tile = jnp.zeros((8, 128), F32)
        for x, at in fields:
            put = (lane == at % 128) | (lane == (at + gap) % 128)
            tile = jnp.where(put, turn(x, at + shift, 1), tile)
        return tile

    def unpacked(tile):
        return stacked([turn(tile, -(FIELD + 2 * layer), 1) for layer in range(LAYERS)])

    def beside(x, ends):
        left = jnp.where(lane == 0, ends, turn(x, 1, x.ndim - 1))
        right = jnp.where(lane == 127, ends, turn(x, -1, x.ndim - 1))
        return left, x, right

    for copy in loads[:first_loads]:
        copy.wait()
    agg_own = jnp.where(core, ag[...], 0)
    own[AGG] = agg_own.astype(F32)
    for k in range(4):
        own[SLOT + k] = jnp.where(core, lk[k], 8).astype(F32)
    moving = [(own[V + i], 2 * i) for i in range(LAYERS)]
    moving += [(own[X + i], FIELD + 2 * i) for i in range(LAYERS)]
    moving += [(own[RATE], 2 * LAYERS)]
    fixed = [(own[AGG], 42), (own[RUB], 44)] + [(own[SLOT + k], 46 + 2 * k) for k in range(4)]
    edge_send[0] = packed(moving + fixed, 1, 1)
    edge_send[1] = packed(moving, 2, 3)
    edge_send[2] = packed([(own[LOAD + i], FIELD + 2 * i) for i in range(LAYERS)], 1, 1)
    pl.semaphore_wait(barrier, len(peers))
    if relayed:
        for k in (REACH, n_py - REACH):
            pl.semaphore_signal(relay, inc=1, device_id=peer(0, k), device_id_type=MESH)
    slot = {(dx, dy): 3 * (dy > 0) + dx + 1 for dx in (-1, 0, 1) for dy in (-1, 1)}
    round1 = []
    for dx in (-1, 1):
        for dy in (-1, 1):
            round1.append(send(edge_send, edge_recv.at[slot[-dx, -dy]], peer(dx, dy)))
    for c in range(2):
        low, high = 4 * c + 1, 4 * c + 2
        for dx, first, second, to in ((1, high, low, 4 * c), (-1, low, high, 4 * c + 3)):
            there = pl.ds(to, 1)
            round1.append(send(own.at[:, pl.ds(first, 1)], near.at[:, there], peer(dx, 0)))
            moved = own.at[pl.ds(0, FAR), pl.ds(second, 1)]
            round1.append(send(moved, far.at[:, there], peer(dx, 0)))
    for dy in (-1, 1):
        round1.append(send(edge_send, edge_recv.at[slot[0, -dy]], peer(0, dy)))

    for copy in loads[first_loads:]:
        copy.wait()
    scale = OMEGA / dg[...]
    weights = [cv[k] * scale for k in range(4)]
    cols = [cc[k] for k in range(4)]
    col_hi = [c >> 7 for c in cols]
    col_lo = [c & 127 for c in cols]
    agg_rows = [agg_own[r : r + 1, :] for r in (1, 2)]
    ids = lax.broadcasted_iota(I32, (128, 128), 0) & (AGG_DEV - 1)
    hot = [(ids == a).astype(F32) for a in agg_rows]

    for copy in round1:
        copy.wait_recv()

    def joined(first, size):
        here = jnp.where(core, own[first : first + size], near[first : first + size])
        return jnp.where(row_ok, here, 0.0)

    def outer(first, size):
        return jnp.where(far_ok, far[first : first + size], 0.0)

    def edges(i):
        shift = -4 if i == 1 else -2

        def both(column):
            left, right = column(0), column(3)
            return jnp.where(side_ok, jnp.where(even, left, turn(right, shift, 1)), 0.0)

        def inner_rows(first):
            below, here, above = (edge_recv[first + j, i] for j in range(3))
            return jnp.where(
                row == 0, turn(below, -2, 0), jnp.where(row == 3, turn(above, 2, 0), here)
            )

        def outer_rows(first):
            below, above = edge_recv[first, i], edge_recv[first + 2, i]
            return jnp.where(row == 0, turn(below, -1, 0), turn(above, 1, 0))

        return (
            jnp.where(row_ok, both(inner_rows), 0.0),
            jnp.where(far_ok, both(outer_rows), 0.0) if i < 2 else None,
        )

    top = (lane == 38) | (lane == 37) | (lane == 102) | (lane == 101)
    bottom = (lane == 0) | (lane == 127) | (lane == 64) | (lane == 63)

    def edge_vertical(tile):
        return jnp.where(top, tile, turn(tile, -2, 1)) - jnp.where(bottom, tile, turn(tile, 2, 1))

    def viscosity(shear, soft):
        axis = shear.ndim - 2
        square = shear * shear
        strain = EPS0 + 0.25 * KZ * (square + turn(square, 4, axis))
        eta = soft * jnp.exp(jnp.log(strain) * (-1.0 / 3.0))
        slope = (-2.0 / 3.0 * 0.25 * KZ) * eta / strain * shear
        return eta, slope

    def derived(slope, shear):
        rise = slope * shear
        return rise + turn(rise, 4, rise.ndim - 2)

    def state(v, x, rate):
        eta, slope = viscosity(vertical(v), rate)
        return (eta, v, x, derived(slope, vertical(x))), slope

    def edge_state(tile):
        shear = edge_vertical(tile)
        eta, slope = viscosity(shear, jnp.where(even, tile[:, 40:41], tile[:, 39:40]))
        slope = turn(slope, FIELD, 1)
        return (turn(eta, FIELD, 1), turn(tile, FIELD, 1), tile, derived(slope, shear)), slope

    def inside(v, x, rate):
        fields = [(v[i], 2 * i) for i in range(LAYERS)]
        fields += [(x[i], FIELD + 2 * i) for i in range(LAYERS)] + [(rate[0], 2 * LAYERS)]
        return packed(fields, 0, -1)

    halo = (joined(V, LAYERS), joined(X, LAYERS), joined(RATE, 1))
    rim = (outer(V, LAYERS), outer(X, LAYERS), outer(RATE, 1))
    here, slope = state(*halo)
    rim_here, _ = state(*rim)
    edge0, rim_edge0 = edges(0)
    edge1, rim_edge1 = edges(1)
    edge_load, _ = edges(2)
    at_edge, edge_slope = edge_state(edge0)
    rim_at_edge, _ = edge_state(rim_edge0)
    past_edge, _ = edge_state(edge1)
    rim_past_edge, _ = edge_state(rim_edge1)
    in_edge, _ = edge_state(inside(*halo))
    rim_in_edge, _ = edge_state(inside(*rim))

    def triples(states, ends):
        found = [beside(a, unpacked(e)) for a, e in zip(states, ends)]
        return [tuple(f[i] for f in found) for i in range(3)]

    def edge_triples(past, at, within):
        left = tuple(jnp.where(even, a, b) for a, b in zip(past, within))
        right = tuple(jnp.where(even, b, a) for a, b in zip(past, within))
        return [left, at, right]

    def halves_of(slots):
        found = []
        for d in range(len(OFFSETS)):
            tally = (slots[0] == d).astype(F32)
            for other in slots[1:]:
                tally = tally + (other == d).astype(F32)
            found.append(0.5 * tally)
        return found

    def coupling(halves, centre, around, beyond, keep):
        eta, v = centre[:2]
        axis = eta.ndim - 2
        side = pull = part = 0.0
        for dx in (-1, 0, 1):
            eta_here, v_here = turn(eta, dx, axis), turn(v, dx, axis)
            sums = [0.0, 0.0, 0.0]
            for d, (ox, oy) in enumerate(OFFSETS):
                if ox != dx:
                    continue
                weight = turn(halves[d], dx, 0)
                if dx != 0:
                    weight = jnp.where(row == (3 if dx < 0 else 0), 0.0, weight)
                eta_n, v_n, x_n, deta_n = around[oy + 1]
                couple = weight * (eta_here + eta_n)
                drop = weight * (v_here - v_n)
                if keep:
                    cs[d] = couple
                    ds_[d] = drop
                sums = [sums[0] + couple, sums[1] + drop, sums[2] + (drop * deta_n - couple * x_n)]
            side, pull, part = (
                old + turn(new, -dx, axis) for old, new in zip((side, pull, part), sums)
            )
        for oy in (-1, 0, 1):
            weight = jnp.where(row == 0, halves[OFFSETS.index((-1, oy))], 0.0)
            weight = jnp.where(row == 3, halves[OFFSETS.index((1, oy))], weight)
            eta_n, v_n, x_n, deta_n = beyond[oy + 1]
            couple = weight * (eta + eta_n)
            drop = weight * (v - v_n)
            side, pull = side + couple, pull + drop
            part = part + (drop * deta_n - couple * x_n)
        return side, pull, part

    eta, v, x, deta = here
    links_here = jnp.where(core, own[SLOT : SLOT + 4], near[SLOT : SLOT + 4])
    rub = jnp.where(core, own[RUB], near[RUB])
    side, pull, part = coupling(
        halves_of([links_here[k] for k in range(4)]),
        here,
        triples(here, at_edge),
        triples(rim_here, rim_at_edge),
        True,
    )
    face = (0.5 * KZ) * (eta[:-1] + eta[1:])
    jump = (0.5 * KZ) * (v[1:] - v[:-1])

    def column_terms(x, deta):
        flux = face * (x[1:] - x[:-1]) + jump * (deta[1:] + deta[:-1])
        return jnp.concatenate([rub * x[:1] - flux[:1], flux[:-1] - flux[1:], flux[-1:]])

    image = side * x + pull * deta + part + column_terms(x, deta)
    img[...] = image
    resid = joined(LOAD, LAYERS) - image

    def of_edge(at):
        return jnp.where(even, edge0[:, at : at + 1], edge0[:, at - 1 : at])

    edge_side, edge_pull, edge_part = coupling(
        halves_of([of_edge(46 + 2 * k) for k in range(4)]),
        at_edge,
        edge_triples(past_edge, at_edge, in_edge),
        edge_triples(rim_past_edge, rim_at_edge, rim_in_edge),
        False,
    )
    eta_e, v_e, x_e, deta_e = at_edge
    edge_rub = of_edge(44)

    def upper_of(tile):
        return turn(tile, -2, 1)

    edge_face = jnp.where(top, 0.0, (0.5 * KZ) * (eta_e + upper_of(eta_e)))
    edge_jump = (0.5 * KZ) * (upper_of(v_e) - v_e)
    flux = edge_face * (upper_of(x_e) - x_e) + edge_jump * (upper_of(deta_e) + deta_e)
    flux = jnp.where(top, 0.0, flux)
    edge_image = edge_side * x_e + edge_pull * deta_e + edge_part - flux
    edge_image = edge_image + jnp.where(bottom, edge_rub * x_e, turn(flux, 2, 1))
    edge_resid = unpacked(edge_load - edge_image)

    side2 = [stacked(pair) for pair in zip(side, unpacked(edge_side))]
    face2 = [stacked(pair) for pair in zip(face, unpacked(edge_face))]
    ends_rub = jnp.where(lane < 64, edge0[:, 44:45], edge0[:, 43:44])
    inverse2, lower2, upper2 = [], [], []
    for layer in range(LAYERS):
        pivot = side2[layer]
        if layer == 0:
            pivot = pivot + stacked([rub, ends_rub]) + face2[0]
        else:
            pivot = pivot + face2[layer - 1] - face2[layer - 1] * upper2[layer - 1]
            if layer < LAYERS - 1:
                pivot = pivot + face2[layer]
        inv = 1.0 / pivot
        inverse2.append(inv)
        lower2.append(face2[layer - 1] * inv if layer else None)
        upper2.append(face2[layer] * inv if layer < LAYERS - 1 else None)

    def line_solve(rhs, inverse, lower, upper):
        forward = [rhs[0] * inverse[0]]
        for layer in range(1, LAYERS):
            forward.append(rhs[layer] * inverse[layer] + lower[layer] * forward[-1])
        back = [forward[-1]]
        for layer in range(LAYERS - 2, -1, -1):
            back.append(forward[layer] + upper[layer] * back[-1])
        return back[::-1]

    solved = line_solve([stacked(p) for p in zip(resid, edge_resid)], inverse2, lower2, upper2)
    inverse = [a[0] for a in inverse2]
    lower = [a if a is None else a[0] for a in lower2]
    upper = [a if a is None else a[0] for a in upper2]
    smooth = jnp.where(row_ok, stacked([a[0] for a in solved]), 0.0)
    ends = jnp.where(row_ok & half_ok, stacked([a[1] for a in solved]), 0.0)

    dsmooth = derived(slope, vertical(smooth))
    dends = derived(unpacked(edge_slope), vertical(ends))
    smooth_beside = beside(smooth, ends)
    dsmooth_beside = beside(dsmooth, dends)
    after = resid - (side * smooth + pull * dsmooth + column_terms(smooth, dsmooth))
    for dx in (-1, 0, 1):
        part = 0.0
        for d, (ox, oy) in enumerate(OFFSETS):
            if ox == dx:
                part = part + (cs[d] * smooth_beside[oy + 1] - ds_[d] * dsmooth_beside[oy + 1])
        after = after + turn(part, -dx, 1)
    mean = jnp.where(core, jnp.sum(after, axis=0) / LAYERS, 0.0)

    sums = [
        lax.dot_general(
            mean, h, (((1,), (1,)), ((), ())),
            precision=lax.Precision.HIGHEST, preferred_element_type=F32,
        )
        for h in hot
    ]
    first = sums[0][1:2] + sums[1][2:3]
    second = sums[0][5:6] + sums[1][6:7]
    mine = jnp.where(lane[0:1] < AGG_DEV, first, second)
    rs[0] = mine
    if relayed:
        pl.semaphore_wait(relay, 2)
    place = lax.rem(py, 2) * n_hi + lax.div(py, 2)
    round3 = []
    for k in sorted(range(1, n_py), key=lambda k: -min(k, n_py - k)):
        round3.append(send(rs, rr.at[pl.ds(place, 1)], peer(0, k)))
    rr[place] = mine

    for d, (dx, _) in enumerate(OFFSETS):
        ws[:, d] = turn(cs[d], -dx, 1)
    rest = line_solve([after[layer] for layer in range(LAYERS)], inverse, lower, upper)
    for layer in range(LAYERS):
        ans[layer] = smooth[layer] + rest[layer]
    held = ws[0] * inverse[0]
    ws[0] = held
    for layer in range(1, LAYERS):
        held = ws[layer] * inverse[layer] + lower[layer] * held
        ws[layer] = held
    for layer in range(LAYERS - 2, -1, -1):
        held = ws[layer] + upper[layer] * held
        ws[layer] = held

    for copy in round3:
        copy.wait_recv()
    evens, odds = rr[0:n_hi, 0, :], rr[n_hi : 2 * n_hi, 0, :]
    low = lax.broadcasted_iota(I32, (n_hi, 128), 1) < AGG_DEV
    target = [
        jnp.where(low, evens, turn(odds, AGG_DEV, 1)) * scale,
        jnp.where(low, turn(evens, AGG_DEV, 1), odds) * scale,
    ]

    def picked(source, at):
        return jnp.take_along_axis(source, at, axis=1, mode="promise_in_bounds")

    iterate = target
    for _ in range(CITERS - 1):
        later = []
        for c in range(2):
            rows = [
                jnp.broadcast_to(iterate[c][h : h + 1], (n_hi, 128)) for h in range(n_hi)
            ]
            value = (1.0 - OMEGA) * iterate[c] + target[c]
            for k in range(4):
                found = picked(rows[0], col_lo[k])
                for h in range(1, n_hi):
                    found = jnp.where(col_hi[k] == h, picked(rows[h], col_lo[k]), found)
                value = value - weights[k] * found
            later.append(value)
        iterate = later
    xs[0] = iterate[0]
    xs[1] = iterate[1]

    def corrected(owner, at):
        h = lax.div(owner, 2)
        source = jnp.where(
            sub < 4,
            jnp.broadcast_to(xs[0, pl.ds(h, 1), :], (8, 128)),
            jnp.broadcast_to(xs[1, pl.ds(h, 1), :], (8, 128)),
        )
        return picked(source, at + AGG_DEV * lax.rem(owner, 2))

    edge_agg = edge0.astype(I32)
    agg_left = jnp.broadcast_to(edge_agg[:, 42:43], (8, 128))
    agg_right = jnp.broadcast_to(edge_agg[:, 41:42], (8, 128))
    corr = corrected(py, agg_own)
    corr_edge = jnp.where(
        lane < 64,
        corrected(wrap(py - 1, n_py), agg_left),
        corrected(wrap(py + 1, n_py), agg_right),
    )
    corr_edge = jnp.where(half_ok, corr_edge, 0.0)
    ct[0] = corr
    ct[1] = corr_edge

    round4 = [send(ct, cr.at[0], peer(1, 0)), send(ct, cr.at[1], peer(-1, 0))]
    for copy in round4:
        copy.wait_recv()

    def rows_joined(i, own):
        joined = jnp.where(
            row == 0, turn(cr[0, i], -2, 0), jnp.where(row == 3, turn(cr[1, i], 2, 0), own)
        )
        return jnp.where(row_ok, joined, 0.0)

    corr_beside = beside(rows_joined(0, corr), rows_joined(1, corr_edge))
    result = ans[...]
    for d, (dx, dy) in enumerate(OFFSETS):
        result = result + ws[:, d] * turn(corr_beside[dy + 1], -dx, 0)
    ans[...] = result
    for copy in round1 + round3 + round4:
        copy.wait_send()


def write_out(image, answer, image_out, answer_out, sems):
    copies = []
    for c in range(2):
        rows = pl.ds(4 * c + 1, 2)
        copies.append(pltpu.make_async_copy(image.at[:, rows], image_out.at[c], sems.at[c]))
        copies.append(pltpu.make_async_copy(answer.at[:, rows], answer_out.at[c], sems.at[2 + c]))
    for copy in copies:
        copy.start()
    for copy in copies:
        copy.wait()


def solution(mesh):
    n_px, n_py = mesh.shape["px"], mesh.shape["py"]
    n_hi = n_py // 2
    n_sends = 14 + (n_py - 1) + 2

    def body(
        velocity, direction, forcing, softness, friction, links, aggregate, diag, vals, cols
    ):
        block = jax.ShapeDtypeStruct(velocity.shape, F32)
        wide = jax.ShapeDtypeStruct((LAYERS, 8, 128), F32)
        results = pl.pallas_call(
            functools.partial(kernel, n_px, n_py),
            out_shape=(wide, wide),
            in_specs=[pl.BlockSpec(memory_space=pltpu.HBM)] * 10,
            out_specs=[pl.BlockSpec(memory_space=pltpu.VMEM)] * 2,
            scratch_shapes=[
                pltpu.VMEM((PLANES, 8, 128), F32),
                pltpu.VMEM((PLANES, 8, 128), F32),
                pltpu.VMEM((FAR, 8, 128), F32),
                pltpu.VMEM((4, 8, 128), I32),
                pltpu.VMEM((8, 128), I32),
                pltpu.VMEM((n_hi, 128), F32),
                pltpu.VMEM((4, n_hi, 128), F32),
                pltpu.VMEM((4, n_hi, 128), I32),
                pltpu.VMEM((3, 8, 128), F32),
                pltpu.VMEM((6, 3, 8, 128), F32),
                pltpu.VMEM((1, 1, 128), F32),
                pltpu.VMEM((n_py, 1, 128), F32),
                pltpu.VMEM((2, n_hi, 128), F32),
                pltpu.VMEM((2, 8, 128), F32),
                pltpu.VMEM((2, 2, 8, 128), F32),
                pltpu.VMEM((8, LAYERS, 8, 128), F32),
                pltpu.VMEM((8, LAYERS, 8, 128), F32),
                pltpu.VMEM((LAYERS, 8, 8, 128), F32),
                pltpu.SemaphoreType.DMA((23,)),
                pltpu.SemaphoreType.DMA((n_sends,)),
                pltpu.SemaphoreType.DMA((n_sends,)),
                pltpu.SemaphoreType.REGULAR,
            ],
            compiler_params=pltpu.CompilerParams(
                collective_id=0, has_side_effects=True, vmem_limit_bytes=32 * 1024 * 1024
            ),
        )(
            *(
                pltpu.with_memory_space_constraint(a, pltpu.HBM)
                for a in (
                    velocity,
                    direction,
                    forcing,
                    softness,
                    friction,
                    links,
                    aggregate,
                    diag.reshape(n_hi, 128),
                    vals.reshape(4, n_hi, 128).transpose(1, 0, 2),
                    cols.reshape(4, n_hi, 128).transpose(1, 0, 2),
                )
            )
        )
        return pl.pallas_call(
            write_out,
            out_shape=(block, block),
            in_specs=[pl.BlockSpec(memory_space=pl.ANY)] * 2,
            out_specs=[pl.BlockSpec(memory_space=pltpu.HBM)] * 2,
            scratch_shapes=[pltpu.SemaphoreType.DMA((4,))],
            compiler_params=pltpu.CompilerParams(vmem_limit_bytes=8 * 1024 * 1024),
        )(*results)

    return jax.shard_map(
        body,
        mesh=mesh,
        in_specs=(
            P(None, None, "px", "py"),
            P(None, None, "px", "py"),
            P(None, None, "px", "py"),
            P("px", "py"),
            P("px", "py"),
            P(None, "px", "py"),
            P("px", "py"),
            P("px"),
            P(None, "px"),
            P(None, "px"),
        ),
        out_specs=(P(None, None, "px", "py"), P(None, None, "px", "py")),
        check_vma=False,
    )
```

time: 42.4 us -> 38.4 us (0.906)
  Pallas kernels: 41.6 us -> 37.6 us
    pallas_call x1, Pallas kernels: 40.9 us -> 36.9 us  [body(): pl.pallas_call(functools.partial(kernel, n_px, n_py), out_shape=(wide, wi...]
where the time goes in v3:
time: 38.4 us; the launch traced here: 38.2 us
  Pallas kernels  37.6 us (98%)
  between operations  0.64 us (2%)
    pallas_call x1, Pallas kernels, body(): pl.pallas_call(functools.partial(kernel, n_px, n_py), out_shape=(wide, wi...  36.9 us

profile of v3, /device:TPU:1, one launch (start us, length us, event | category | flops | bytes accessed | tf_op | source)
XLA Modules:
  0.0 38.2 jit_solution(12452278875408822264)
XLA Ops:
  0.6 36.9 %shard_map.113 = (f32[20,8,128]{2,1,0:T(8,128)S(1)}, f32[20,8,128]{2,1,0:T(8,128)S(1)}) custom-call(f32[2,20,2,128]{3,2,1,0:T(2,128)} %velocity.1, f32[2,20,2,128]{3,2,1,0:T(2,128)} %direction.1, f32[2,20,2,128]{3,2,1,0:T(2,128)} %forcing.1, f32[2,128]{1,0:T(2,128)} %softness.1, f32[2,128]{1,0:T(2,128)} %friction.1, s32[4,2,128]{2,1,0:T(2,128)} %links.1, ...), custom_call_target="tpu_custom_call" | custom-call | tf_op jit(solution)/shard_map/pallas_call | solution.py:554
  37.6 0.7 %shard_map.114 = (f32[2,20,2,128]{3,2,1,0:T(2,128)}, f32[2,20,2,128]{3,2,1,0:T(2,128)}) custom-call(f32[20,8,128]{2,1,0:T(8,128)S(1)} %get-tuple-element.4.image, f32[20,8,128]{2,1,0:T(8,128)S(1)} %get-tuple-element.5.answer), custom_call_target="tpu_custom_call" | custom-call | tf_op jit(solution)/shard_map/pallas_call | solution.py:603

commit v4 on v3

--- a/solution.py
+++ b/solution.py
@@ -57,23 +57,24 @@
     far,
     lk,
     ag,
-    dg,
-    cv,
+    cf,
     cc,
+    cf_near,
+    cc_near,
     edge_send,
     edge_recv,
     rs,
     rr,
     xs,
-    ct,
-    cr,
     cs,
     ds_,
     ws,
     load_sem,
     send_sem,
     recv_sem,
+    gather_sem,
     relay,
+    complete,
 ):
     px = lax.axis_index("px")
     py = lax.axis_index("py")
@@ -85,11 +86,23 @@
     def peer(dx, dy):
         return (wrap(px + dx, n_px), wrap(py + dy, n_py))
 
-    around = [peer(dx, dy) for dx in (-1, 1) for dy in (-1, 1, 0)]
-    peers = around + [peer(0, k) for k in range(1, n_py) if min(k, n_py - k) <= REACH]
+    def inside_grid(dx, dy):
+        ok = (px >= 0) if dx == 0 else (px > 0) if dx < 0 else (px < n_px - 1)
+        return ok if dy == 0 else ok & ((py > 0) if dy < 0 else (py < n_py - 1))
+
     barrier = pltpu.get_barrier_semaphore()
-    for target in peers:
-        pl.semaphore_signal(barrier, inc=1, device_id=target, device_id_type=MESH)
+
+    def greet(dx, dy):
+        pl.semaphore_signal(barrier, inc=1, device_id=peer(dx, dy), device_id_type=MESH)
+
+    line = [k for k in range(1, n_py) if min(k, n_py - k) <= REACH]
+    expected = len(line)
+    for dx in (-1, 1):
+        for dy in (-1, 1, 0):
+            pl.when(inside_grid(dx, dy))(functools.partial(greet, dx, dy))
+            expected = expected + jnp.where(inside_grid(dx, dy), 1, 0)
+    for k in line:
+        greet(0, k)
     relayed = n_py // 2 > REACH
 
     loads = []
@@ -109,9 +122,9 @@
         load(links, lk.at[:, rows])
         load(aggregate, ag.at[rows])
     first_loads = len(loads)
-    load(coarse_diag, dg)
+    load(coarse_diag, cf.at[0])
     for k in range(4):
-        load(coarse_vals.at[:, k], cv.at[k])
+        load(coarse_vals.at[:, k], cf.at[1 + k])
         load(coarse_cols.at[:, k], cc.at[k])
 
     lane = lax.broadcasted_iota(I32, (8, 128), 1)
@@ -132,7 +145,7 @@
 
     count = [0]
 
-    def send(src, dst, target):
+    def send(src, dst, target, step=(0, 0)):
         i = count[0]
         count[0] += 1
         copy = pltpu.make_async_remote_copy(
@@ -143,8 +156,25 @@
             device_id=target,
             device_id_type=MESH,
         )
-        copy.start()
-        return copy
+        if step == (0, 0):
+            copy.start()
+        else:
+            pl.when(inside_grid(*step))(copy.start)
+        return copy, step
+
+    def received(copies):
+        for copy, (dx, dy) in copies:
+            if (dx, dy) == (0, 0):
+                copy.wait_recv()
+            else:
+                pl.when(inside_grid(-dx, -dy))(copy.wait_recv)
+
+    def sent(copies):
+        for copy, step in copies:
+            if step == (0, 0):
+                copy.wait_send()
+            else:
+                pl.when(inside_grid(*step))(copy.wait_send)
 
     def packed(fields, shift, gap):
         tile = jnp.zeros((8, 128), F32)
@@ -174,38 +204,49 @@
     edge_send[0] = packed(moving + fixed, 1, 1)
     edge_send[1] = packed(moving, 2, 3)
     edge_send[2] = packed([(own[LOAD + i], FIELD + 2 * i) for i in range(LAYERS)], 1, 1)
-    pl.semaphore_wait(barrier, len(peers))
+    pl.semaphore_wait(barrier, expected)
     if relayed:
         for k in (REACH, n_py - REACH):
             pl.semaphore_signal(relay, inc=1, device_id=peer(0, k), device_id_type=MESH)
     slot = {(dx, dy): 3 * (dy > 0) + dx + 1 for dx in (-1, 0, 1) for dy in (-1, 1)}
     round1 = []
+    def send_round1(src, dst, dx, dy):
+        round1.append(send(src, dst, peer(dx, dy), (dx, dy)))
+
     for dx in (-1, 1):
         for dy in (-1, 1):
-            round1.append(send(edge_send, edge_recv.at[slot[-dx, -dy]], peer(dx, dy)))
+            send_round1(edge_send, edge_recv.at[slot[-dx, -dy]], dx, dy)
     for c in range(2):
         low, high = 4 * c + 1, 4 * c + 2
         for dx, first, second, to in ((1, high, low, 4 * c), (-1, low, high, 4 * c + 3)):
             there = pl.ds(to, 1)
-            round1.append(send(own.at[:, pl.ds(first, 1)], near.at[:, there], peer(dx, 0)))
+            send_round1(own.at[:, pl.ds(first, 1)], near.at[:, there], dx, 0)
             moved = own.at[pl.ds(0, FAR), pl.ds(second, 1)]
-            round1.append(send(moved, far.at[:, there], peer(dx, 0)))
+            send_round1(moved, far.at[:, there], dx, 0)
     for dy in (-1, 1):
-        round1.append(send(edge_send, edge_recv.at[slot[0, -dy]], peer(0, dy)))
+        send_round1(edge_send, edge_recv.at[slot[0, -dy]], 0, dy)
 
     for copy in loads[first_loads:]:
         copy.wait()
-    scale = OMEGA / dg[...]
-    weights = [cv[k] * scale for k in range(4)]
-    cols = [cc[k] for k in range(4)]
-    col_hi = [c >> 7 for c in cols]
-    col_lo = [c & 127 for c in cols]
+    coarse = []
+    for dx, i in ((1, 0), (-1, 1)):
+        coarse.append(send(cf, cf_near.at[i], peer(dx, 0), (dx, 0)))
+        coarse.append(send(cc, cc_near.at[i], peer(dx, 0), (dx, 0)))
+    if relayed:
+        pl.semaphore_wait(relay, 2)
+    lines = 0
+    for dx in (-1, 1):
+
+        def tell(dx=dx):
+            pl.semaphore_signal(complete, inc=1, device_id=peer(dx, 0), device_id_type=MESH)
+
+        pl.when(inside_grid(dx, 0))(tell)
+        lines = lines + jnp.where(inside_grid(dx, 0), 1, 0)
     agg_rows = [agg_own[r : r + 1, :] for r in (1, 2)]
     ids = lax.broadcasted_iota(I32, (128, 128), 0) & (AGG_DEV - 1)
     hot = [(ids == a).astype(F32) for a in agg_rows]
 
-    for copy in round1:
-        copy.wait_recv()
+    received(round1)
 
     def joined(first, size):
         here = jnp.where(core, own[first : first + size], near[first : first + size])
@@ -436,13 +477,38 @@
     second = sums[0][5:6] + sums[1][6:7]
     mine = jnp.where(lane[0:1] < AGG_DEV, first, second)
     rs[0] = mine
-    if relayed:
-        pl.semaphore_wait(relay, 2)
     place = lax.rem(py, 2) * n_hi + lax.div(py, 2)
-    round3 = []
-    for k in sorted(range(1, n_py), key=lambda k: -min(k, n_py - k)):
-        round3.append(send(rs, rr.at[pl.ds(place, 1)], peer(0, k)))
-    rr[place] = mine
+
+    def push(dx, k):
+        group = 1 - dx
+        pltpu.make_async_remote_copy(
+            src_ref=rs,
+            dst_ref=rr.at[pl.ds(group * n_py + place, 1)],
+            send_sem=gather_sem.at[1 + dx],
+            recv_sem=gather_sem.at[3 + group],
+            device_id=peer(dx, k),
+            device_id_type=MESH,
+        ).start()
+
+    pl.semaphore_wait(complete, lines)
+    for reach in range(n_py // 2, -1, -1):
+        far_off = sorted({reach, (n_py - reach) % n_py})
+        for dx in (-1, 1):
+
+            def push_all(dx=dx, far_off=far_off):
+                for k in far_off:
+                    push(dx, k)
+
+            pl.when(inside_grid(dx, 0))(push_all)
+        for k in far_off:
+            if k:
+                push(0, k)
+    kept = pltpu.make_async_copy(rs, rr.at[pl.ds(n_py + place, 1)], gather_sem.at[4])
+    kept.start()
+
+    def gathered(sem, first, size):
+        some = rr.at[pl.ds(first, size)]
+        pltpu.make_async_copy(some, some, gather_sem.at[sem]).wait()
 
     for d, (dx, _) in enumerate(OFFSETS):
         ws[:, d] = turn(cs[d], -dx, 1)
@@ -458,75 +524,75 @@
         held = ws[layer] + upper[layer] * held
         ws[layer] = held
 
-    for copy in round3:
-        copy.wait_recv()
-    evens, odds = rr[0:n_hi, 0, :], rr[n_hi : 2 * n_hi, 0, :]
+    received(coarse)
+    operators = []
+    for f, c in ((cf_near.at[0], cc_near.at[0]), (cf, cc), (cf_near.at[1], cc_near.at[1])):
+        scale = OMEGA / f[0]
+        cols = [c[k] for k in range(4)]
+        weights = [f[1 + k] * scale for k in range(4)]
+        operators.append((scale, weights, [a >> 7 for a in cols], [a & 127 for a in cols]))
+    agg_all = jnp.where(core, own[AGG], near[AGG])
+    agg_all = jnp.where(row_ok, agg_all, 0.0).astype(I32)
+    sent(round1 + coarse)
+    gathered(4, n_py, n_py)
+    pl.when(inside_grid(-1, 0))(lambda: gathered(3, 0, n_py))
+    pl.when(inside_grid(1, 0))(lambda: gathered(5, 2 * n_py, n_py))
     low = lax.broadcasted_iota(I32, (n_hi, 128), 1) < AGG_DEV
-    target = [
-        jnp.where(low, evens, turn(odds, AGG_DEV, 1)) * scale,
-        jnp.where(low, turn(evens, AGG_DEV, 1), odds) * scale,
-    ]
 
     def picked(source, at):
         return jnp.take_along_axis(source, at, axis=1, mode="promise_in_bounds")
 
-    iterate = target
-    for _ in range(CITERS - 1):
-        later = []
-        for c in range(2):
-            rows = [
-                jnp.broadcast_to(iterate[c][h : h + 1], (n_hi, 128)) for h in range(n_hi)
-            ]
-            value = (1.0 - OMEGA) * iterate[c] + target[c]
-            for k in range(4):
-                found = picked(rows[0], col_lo[k])
-                for h in range(1, n_hi):
-                    found = jnp.where(col_hi[k] == h, picked(rows[h], col_lo[k]), found)
-                value = value - weights[k] * found
-            later.append(value)
-        iterate = later
-    xs[0] = iterate[0]
-    xs[1] = iterate[1]
+    for g, (scale, weights, col_hi, col_lo) in enumerate(operators):
+        evens = rr[g * n_py : g * n_py + n_hi, 0, :]
+        odds = rr[g * n_py + n_hi : (g + 1) * n_py, 0, :]
+        target = [
+            jnp.where(low, evens, turn(odds, AGG_DEV, 1)) * scale,
+            jnp.where(low, turn(evens, AGG_DEV, 1), odds) * scale,
+        ]
+        iterate = target
+        for _ in range(CITERS - 1):
+            later = []
+            for c in range(2):
+                rows = [
+                    jnp.broadcast_to(iterate[c][h : h + 1], (n_hi, 128)) for h in range(n_hi)
+                ]
+                value = (1.0 - OMEGA) * iterate[c] + target[c]
+                for k in range(4):
+                    found = picked(rows[0], col_lo[k])
+                    for h in range(1, n_hi):
+                        found = jnp.where(col_hi[k] == h, picked(rows[h], col_lo[k]), found)
+                    value = value - weights[k] * found
+                later.append(value)
+            iterate = later
+        xs[g, 0] = iterate[0]
+        xs[g, 1] = iterate[1]
 
     def corrected(owner, at):
-        h = lax.div(owner, 2)
-        source = jnp.where(
-            sub < 4,
-            jnp.broadcast_to(xs[0, pl.ds(h, 1), :], (8, 128)),
-            jnp.broadcast_to(xs[1, pl.ds(h, 1), :], (8, 128)),
-        )
+        h = pl.ds(lax.div(owner, 2), 1)
+        source = None
+        for g in range(3):
+            line = jnp.where(sub < 4, xs[g, 0, h, :], xs[g, 1, h, :])
+            source = line if g == 0 else jnp.where(row >= (1 if g == 1 else 3), line, source)
         return picked(source, at + AGG_DEV * lax.rem(owner, 2))
 
     edge_agg = edge0.astype(I32)
     agg_left = jnp.broadcast_to(edge_agg[:, 42:43], (8, 128))
     agg_right = jnp.broadcast_to(edge_agg[:, 41:42], (8, 128))
-    corr = corrected(py, agg_own)
+    corr = jnp.where(row_ok, corrected(py, agg_all), 0.0)
     corr_edge = jnp.where(
-        lane < 64,
+        half == 0,
         corrected(wrap(py - 1, n_py), agg_left),
         corrected(wrap(py + 1, n_py), agg_right),
     )
-    corr_edge = jnp.where(half_ok, corr_edge, 0.0)
-    ct[0] = corr
-    ct[1] = corr_edge
-
-    round4 = [send(ct, cr.at[0], peer(1, 0)), send(ct, cr.at[1], peer(-1, 0))]
-    for copy in round4:
-        copy.wait_recv()
-
-    def rows_joined(i, own):
-        joined = jnp.where(
-            row == 0, turn(cr[0, i], -2, 0), jnp.where(row == 3, turn(cr[1, i], 2, 0), own)
-        )
-        return jnp.where(row_ok, joined, 0.0)
-
-    corr_beside = beside(rows_joined(0, corr), rows_joined(1, corr_edge))
+    corr_edge = jnp.where(row_ok & half_ok, corr_edge, 0.0)
+    corr_beside = beside(corr, corr_edge)
     result = ans[...]
     for d, (dx, dy) in enumerate(OFFSETS):
         result = result + ws[:, d] * turn(corr_beside[dy + 1], -dx, 0)
     ans[...] = result
-    for copy in round1 + round3 + round4:
-        copy.wait_send()
+    gathered(1, 0, n_py - 1)
+    pl.when(inside_grid(-1, 0))(lambda: gathered(0, 0, n_py))
+    pl.when(inside_grid(1, 0))(lambda: gathered(2, 0, n_py))
 
 
 def write_out(image, answer, image_out, answer_out, sems):
@@ -544,7 +610,7 @@
 def solution(mesh):
     n_px, n_py = mesh.shape["px"], mesh.shape["py"]
     n_hi = n_py // 2
-    n_sends = 14 + (n_py - 1) + 2
+    n_sends = 18
 
     def body(
         velocity, direction, forcing, softness, friction, links, aggregate, diag, vals, cols
@@ -562,22 +628,23 @@
                 pltpu.VMEM((FAR, 8, 128), F32),
                 pltpu.VMEM((4, 8, 128), I32),
                 pltpu.VMEM((8, 128), I32),
-                pltpu.VMEM((n_hi, 128), F32),
-                pltpu.VMEM((4, n_hi, 128), F32),
+                pltpu.VMEM((5, n_hi, 128), F32),
                 pltpu.VMEM((4, n_hi, 128), I32),
+                pltpu.VMEM((2, 5, n_hi, 128), F32),
+                pltpu.VMEM((2, 4, n_hi, 128), I32),
                 pltpu.VMEM((3, 8, 128), F32),
                 pltpu.VMEM((6, 3, 8, 128), F32),
                 pltpu.VMEM((1, 1, 128), F32),
-                pltpu.VMEM((n_py, 1, 128), F32),
-                pltpu.VMEM((2, n_hi, 128), F32),
-                pltpu.VMEM((2, 8, 128), F32),
-                pltpu.VMEM((2, 2, 8, 128), F32),
+                pltpu.VMEM((3 * n_py, 1, 128), F32),
+                pltpu.VMEM((3, 2, n_hi, 128), F32),
                 pltpu.VMEM((8, LAYERS, 8, 128), F32),
                 pltpu.VMEM((8, LAYERS, 8, 128), F32),
                 pltpu.VMEM((LAYERS, 8, 8, 128), F32),
                 pltpu.SemaphoreType.DMA((23,)),
                 pltpu.SemaphoreType.DMA((n_sends,)),
                 pltpu.SemaphoreType.DMA((n_sends,)),
+                pltpu.SemaphoreType.DMA((6,)),
+                pltpu.SemaphoreType.REGULAR,
                 pltpu.SemaphoreType.REGULAR,
             ],
             compiler_params=pltpu.CompilerParams(

time: 38.4 us -> 36.5 us (0.951)
  the two profiles are of different devices: /device:TPU:1 before, /device:TPU:32 now
where the time goes in v4:
time: 36.5 us; the launch traced here: 36.3 us
  Pallas kernels  35.6 us (98%)
  between operations  0.64 us (2%)
    pallas_call x1, Pallas kernels, body(): pl.pallas_call(functools.partial(kernel, n_px, n_py), out_shape=(wide, wi...  35 us

profile of v4, /device:TPU:32, one launch (start us, length us, event | category | flops | bytes accessed | tf_op | source)
XLA Modules:
  0.0 36.3 jit_solution(14027286261515748411)
XLA Ops:
  0.6 35.0 %shard_map.113 = (f32[20,8,128]{2,1,0:T(8,128)S(1)}, f32[20,8,128]{2,1,0:T(8,128)S(1)}) custom-call(f32[2,20,2,128]{3,2,1,0:T(2,128)} %velocity.1, f32[2,20,2,128]{3,2,1,0:T(2,128)} %direction.1, f32[2,20,2,128]{3,2,1,0:T(2,128)} %forcing.1, f32[2,128]{1,0:T(2,128)} %softness.1, f32[2,128]{1,0:T(2,128)} %friction.1, s32[4,2,128]{2,1,0:T(2,128)} %links.1, ...), custom_call_target="tpu_custom_call" | custom-call | tf_op jit(solution)/shard_map/pallas_call | solution.py:620
  35.6 0.7 %shard_map.114 = (f32[2,20,2,128]{3,2,1,0:T(2,128)}, f32[2,20,2,128]{3,2,1,0:T(2,128)}) custom-call(f32[20,8,128]{2,1,0:T(8,128)S(1)} %get-tuple-element.4.image, f32[20,8,128]{2,1,0:T(8,128)S(1)} %get-tuple-element.5.answer), custom_call_target="tpu_custom_call" | custom-call | tf_op jit(solution)/shard_map/pallas_call | solution.py:670

commit v5 on v4

--- a/solution.py
+++ b/solution.py
@@ -145,7 +145,7 @@
 
     count = [0]
 
-    def send(src, dst, target, step=(0, 0)):
+    def send(src, dst, target, to_ok, from_ok):
         i = count[0]
         count[0] += 1
         copy = pltpu.make_async_remote_copy(
@@ -156,25 +156,16 @@
             device_id=target,
             device_id_type=MESH,
         )
-        if step == (0, 0):
-            copy.start()
-        else:
-            pl.when(inside_grid(*step))(copy.start)
-        return copy, step
+        pl.when(to_ok)(copy.start)
+        return copy, to_ok, from_ok
 
     def received(copies):
-        for copy, (dx, dy) in copies:
-            if (dx, dy) == (0, 0):
-                copy.wait_recv()
-            else:
-                pl.when(inside_grid(-dx, -dy))(copy.wait_recv)
+        for copy, _, from_ok in copies:
+            pl.when(from_ok)(copy.wait_recv)
 
     def sent(copies):
-        for copy, step in copies:
-            if step == (0, 0):
-                copy.wait_send()
-            else:
-                pl.when(inside_grid(*step))(copy.wait_send)
+        for copy, to_ok, _ in copies:
+            pl.when(to_ok)(copy.wait_send)
 
     def packed(fields, shift, gap):
         tile = jnp.zeros((8, 128), F32)
@@ -211,7 +202,8 @@
     slot = {(dx, dy): 3 * (dy > 0) + dx + 1 for dx in (-1, 0, 1) for dy in (-1, 1)}
     round1 = []
     def send_round1(src, dst, dx, dy):
-        round1.append(send(src, dst, peer(dx, dy), (dx, dy)))
+        to_ok, from_ok = inside_grid(dx, dy), inside_grid(-dx, -dy)
+        round1.append(send(src, dst, peer(dx, dy), to_ok, from_ok))
 
     for dx in (-1, 1):
         for dy in (-1, 1):
@@ -226,12 +218,16 @@
     for dy in (-1, 1):
         send_round1(edge_send, edge_recv.at[slot[0, -dy]], 0, dy)
 
+    odd = lax.rem(px, 2)
+    pairs = []
+    for dx in (1 - 2 * odd, 2 * odd - 1):
+        pairs.append((dx, (px + dx >= 0) & (px + dx < n_px)))
     for copy in loads[first_loads:]:
         copy.wait()
     coarse = []
-    for dx, i in ((1, 0), (-1, 1)):
-        coarse.append(send(cf, cf_near.at[i], peer(dx, 0), (dx, 0)))
-        coarse.append(send(cc, cc_near.at[i], peer(dx, 0), (dx, 0)))
+    for i, (dx, ok) in enumerate(pairs):
+        coarse.append(send(cf, cf_near.at[i], peer(dx, 0), ok, ok))
+        coarse.append(send(cc, cc_near.at[i], peer(dx, 0), ok, ok))
     if relayed:
         pl.semaphore_wait(relay, 2)
     lines = 0
@@ -423,33 +419,50 @@
     side2 = [stacked(pair) for pair in zip(side, unpacked(edge_side))]
     face2 = [stacked(pair) for pair in zip(face, unpacked(edge_face))]
     ends_rub = jnp.where(lane < 64, edge0[:, 44:45], edge0[:, 43:44])
-    inverse2, lower2, upper2 = [], [], []
-    for layer in range(LAYERS):
+    middle = LAYERS // 2
+    inverse2, inward2, outward2 = [None] * LAYERS, [None] * LAYERS, [None] * LAYERS
+
+    def eliminate(layer, before, after):
         pivot = side2[layer]
         if layer == 0:
-            pivot = pivot + stacked([rub, ends_rub]) + face2[0]
-        else:
-            pivot = pivot + face2[layer - 1] - face2[layer - 1] * upper2[layer - 1]
-            if layer < LAYERS - 1:
-                pivot = pivot + face2[layer]
+            pivot = pivot + stacked([rub, ends_rub])
+        if after is not None:
+            pivot = pivot + face2[after]
+        if before is not None:
+            previous = layer - 1 if layer < middle else layer + 1
+            pivot = pivot + face2[before] - face2[before] * outward2[previous]
         inv = 1.0 / pivot
-        inverse2.append(inv)
-        lower2.append(face2[layer - 1] * inv if layer else None)
-        upper2.append(face2[layer] * inv if layer < LAYERS - 1 else None)
-
-    def line_solve(rhs, inverse, lower, upper):
-        forward = [rhs[0] * inverse[0]]
-        for layer in range(1, LAYERS):
-            forward.append(rhs[layer] * inverse[layer] + lower[layer] * forward[-1])
-        back = [forward[-1]]
-        for layer in range(LAYERS - 2, -1, -1):
-            back.append(forward[layer] + upper[layer] * back[-1])
-        return back[::-1]
-
-    solved = line_solve([stacked(p) for p in zip(resid, edge_resid)], inverse2, lower2, upper2)
-    inverse = [a[0] for a in inverse2]
-    lower = [a if a is None else a[0] for a in lower2]
-    upper = [a if a is None else a[0] for a in upper2]
+        inverse2[layer] = inv
+        inward2[layer] = None if before is None else face2[before] * inv
+        outward2[layer] = None if after is None else face2[after] * inv
+
+    for step in range(middle):
+        eliminate(step, step - 1 if step else None, step)
+        layer = LAYERS - 1 - step
+        eliminate(layer, layer if step else None, layer - 1)
+    meet2 = 1.0 / (1.0 - outward2[middle - 1] * outward2[middle])
+
+    def line_solve(rhs, inverse, inward, outward, meet):
+        found = [None] * LAYERS
+        for step in range(middle):
+            for layer, previous in ((step, step - 1), (LAYERS - 1 - step, LAYERS - step)):
+                found[layer] = rhs[layer] * inverse[layer]
+                if step:
+                    found[layer] = found[layer] + inward[layer] * found[previous]
+        low, high = middle - 1, middle
+        found[low] = (found[low] + outward[low] * found[high]) * meet
+        found[high] = found[high] + outward[high] * found[low]
+        for step in range(1, middle):
+            for layer, previous in ((low - step, low - step + 1), (high + step, high + step - 1)):
+                found[layer] = found[layer] + outward[layer] * found[previous]
+        return found
+
+    solved = line_solve(
+        [stacked(p) for p in zip(resid, edge_resid)], inverse2, inward2, outward2, meet2
+    )
+    own_factors = [
+        [a if a is None else a[0] for a in factor] for factor in (inverse2, inward2, outward2)
+    ] + [meet2[0]]
     smooth = jnp.where(row_ok, stacked([a[0] for a in solved]), 0.0)
     ends = jnp.where(row_ok & half_ok, stacked([a[1] for a in solved]), 0.0)
 
@@ -457,34 +470,43 @@
     dends = derived(unpacked(edge_slope), vertical(ends))
     smooth_beside = beside(smooth, ends)
     dsmooth_beside = beside(dsmooth, dends)
-    after = resid - (side * smooth + pull * dsmooth + column_terms(smooth, dsmooth))
+    plain = resid - (side * smooth + pull * dsmooth)
+    parts = []
     for dx in (-1, 0, 1):
         part = 0.0
         for d, (ox, oy) in enumerate(OFFSETS):
             if ox == dx:
                 part = part + (cs[d] * smooth_beside[oy + 1] - ds_[d] * dsmooth_beside[oy + 1])
-        after = after + turn(part, -dx, 1)
-    mean = jnp.where(core, jnp.sum(after, axis=0) / LAYERS, 0.0)
-
-    sums = [
-        lax.dot_general(
-            mean, h, (((1,), (1,)), ((), ())),
-            precision=lax.Precision.HIGHEST, preferred_element_type=F32,
-        )
-        for h in hot
-    ]
-    first = sums[0][1:2] + sums[1][2:3]
-    second = sums[0][5:6] + sums[1][6:7]
-    mine = jnp.where(lane[0:1] < AGG_DEV, first, second)
+        parts.append(part)
+    total = jnp.sum(plain, axis=0) - rub * smooth[0]
+    for dx, part in zip((-1, 0, 1), parts):
+        total = total + turn(jnp.sum(part, axis=0), -dx, 0)
+    mean = jnp.where(core, total / LAYERS, 0.0)
+
+    pieces, rest_of = [], mean
+    for _ in range(2):
+        large = rest_of * 65537.0
+        piece = large - (large - rest_of)
+        pieces.append(piece)
+        rest_of = rest_of - piece
+    pieces.append(rest_of)
+    pieces = jnp.concatenate(pieces, axis=0)
+    sums = lax.dot_general(
+        jnp.concatenate([pieces, turn(pieces, -1, 0)], axis=1),
+        jnp.concatenate(hot, axis=1),
+        (((1,), (1,)), ((), ())),
+        preferred_element_type=F32,
+    )
+    sums = sums[0:8] + sums[8:16] + sums[16:24]
+    mine = jnp.where(lane[0:1] < AGG_DEV, sums[1:2], sums[5:6])
     rs[0] = mine
     place = lax.rem(py, 2) * n_hi + lax.div(py, 2)
 
-    def push(dx, k):
-        group = 1 - dx
+    def push(group, dx, k):
         pltpu.make_async_remote_copy(
             src_ref=rs,
             dst_ref=rr.at[pl.ds(group * n_py + place, 1)],
-            send_sem=gather_sem.at[1 + dx],
+            send_sem=gather_sem.at[group],
             recv_sem=gather_sem.at[3 + group],
             device_id=peer(dx, k),
             device_id_type=MESH,
@@ -493,40 +515,38 @@
     pl.semaphore_wait(complete, lines)
     for reach in range(n_py // 2, -1, -1):
         far_off = sorted({reach, (n_py - reach) % n_py})
-        for dx in (-1, 1):
-
-            def push_all(dx=dx, far_off=far_off):
+        for group in (2, 1):
+            dx, ok = pairs[group - 1]
+
+            def push_all(group=group, dx=dx, far_off=far_off):
                 for k in far_off:
-                    push(dx, k)
-
-            pl.when(inside_grid(dx, 0))(push_all)
+                    push(group, dx, k)
+
+            pl.when(ok)(push_all)
         for k in far_off:
             if k:
-                push(0, k)
-    kept = pltpu.make_async_copy(rs, rr.at[pl.ds(n_py + place, 1)], gather_sem.at[4])
+                push(0, 0, k)
+    kept = pltpu.make_async_copy(rs, rr.at[pl.ds(place, 1)], gather_sem.at[3])
     kept.start()
 
     def gathered(sem, first, size):
         some = rr.at[pl.ds(first, size)]
         pltpu.make_async_copy(some, some, gather_sem.at[sem]).wait()
 
+    after = plain - column_terms(smooth, dsmooth)
+    for dx, part in zip((-1, 0, 1), parts):
+        after = after + turn(part, -dx, 1)
+    rest = line_solve([after[layer] for layer in range(LAYERS)], *own_factors)
+    for layer in range(LAYERS):
+        ans[layer] = smooth[layer] + rest[layer]
     for d, (dx, _) in enumerate(OFFSETS):
         ws[:, d] = turn(cs[d], -dx, 1)
-    rest = line_solve([after[layer] for layer in range(LAYERS)], inverse, lower, upper)
-    for layer in range(LAYERS):
-        ans[layer] = smooth[layer] + rest[layer]
-    held = ws[0] * inverse[0]
-    ws[0] = held
-    for layer in range(1, LAYERS):
-        held = ws[layer] * inverse[layer] + lower[layer] * held
-        ws[layer] = held
-    for layer in range(LAYERS - 2, -1, -1):
-        held = ws[layer] + upper[layer] * held
+    for layer, held in enumerate(line_solve([ws[i] for i in range(LAYERS)], *own_factors)):
         ws[layer] = held
 
     received(coarse)
     operators = []
-    for f, c in ((cf_near.at[0], cc_near.at[0]), (cf, cc), (cf_near.at[1], cc_near.at[1])):
+    for f, c in ((cf, cc), (cf_near.at[0], cc_near.at[0]), (cf_near.at[1], cc_near.at[1])):
         scale = OMEGA / f[0]
         cols = [c[k] for k in range(4)]
         weights = [f[1 + k] * scale for k in range(4)]
@@ -534,15 +554,16 @@
     agg_all = jnp.where(core, own[AGG], near[AGG])
     agg_all = jnp.where(row_ok, agg_all, 0.0).astype(I32)
     sent(round1 + coarse)
-    gathered(4, n_py, n_py)
-    pl.when(inside_grid(-1, 0))(lambda: gathered(3, 0, n_py))
-    pl.when(inside_grid(1, 0))(lambda: gathered(5, 2 * n_py, n_py))
     low = lax.broadcasted_iota(I32, (n_hi, 128), 1) < AGG_DEV
 
     def picked(source, at):
         return jnp.take_along_axis(source, at, axis=1, mode="promise_in_bounds")
 
     for g, (scale, weights, col_hi, col_lo) in enumerate(operators):
+        if g == 0:
+            gathered(3, 0, n_py)
+        else:
+            pl.when(pairs[g - 1][1])(functools.partial(gathered, 3 + g, g * n_py, n_py))
         evens = rr[g * n_py : g * n_py + n_hi, 0, :]
         odds = rr[g * n_py + n_hi : (g + 1) * n_py, 0, :]
         target = [
@@ -569,10 +590,10 @@
 
     def corrected(owner, at):
         h = pl.ds(lax.div(owner, 2), 1)
-        source = None
-        for g in range(3):
-            line = jnp.where(sub < 4, xs[g, 0, h, :], xs[g, 1, h, :])
-            source = line if g == 0 else jnp.where(row >= (1 if g == 1 else 3), line, source)
+        below, here, above = (
+            jnp.where(sub < 4, xs[g, 0, h, :], xs[g, 1, h, :]) for g in (2 - odd, 0, 1 + odd)
+        )
+        source = jnp.where(row == 0, below, jnp.where(row == 3, above, here))
         return picked(source, at + AGG_DEV * lax.rem(owner, 2))
 
     edge_agg = edge0.astype(I32)
@@ -590,9 +611,9 @@
     for d, (dx, dy) in enumerate(OFFSETS):
         result = result + ws[:, d] * turn(corr_beside[dy + 1], -dx, 0)
     ans[...] = result
-    gathered(1, 0, n_py - 1)
-    pl.when(inside_grid(-1, 0))(lambda: gathered(0, 0, n_py))
-    pl.when(inside_grid(1, 0))(lambda: gathered(2, 0, n_py))
+    gathered(0, 0, n_py - 1)
+    for group, (_, ok) in enumerate(pairs):
+        pl.when(ok)(functools.partial(gathered, 1 + group, 0, n_py))
 
 
 def write_out(image, answer, image_out, answer_out, sems):

time: 36.5 us -> 35.6 us (0.975)
  the two profiles are of different devices: /device:TPU:32 before, /device:TPU:31 now
where the time goes in v5:
time: 35.6 us; the launch traced here: 35.1 us
  Pallas kernels  34.5 us (97%)
  between operations  0.64 us (2%)
    pallas_call x1, Pallas kernels, body(): pl.pallas_call(functools.partial(kernel, n_px, n_py), out_shape=(wide, wi...  33.8 us

profile of v5, /device:TPU:31, one launch (start us, length us, event | category | flops | bytes accessed | tf_op | source)
XLA Modules:
  0.0 35.1 jit_solution(14975337703181101171)
XLA Ops:
  0.6 33.8 %shard_map.113 = (f32[20,8,128]{2,1,0:T(8,128)S(1)}, f32[20,8,128]{2,1,0:T(8,128)S(1)}) custom-call(f32[2,20,2,128]{3,2,1,0:T(2,128)} %velocity.1, f32[2,20,2,128]{3,2,1,0:T(2,128)} %direction.1, f32[2,20,2,128]{3,2,1,0:T(2,128)} %forcing.1, f32[2,128]{1,0:T(2,128)} %softness.1, f32[2,128]{1,0:T(2,128)} %friction.1, s32[4,2,128]{2,1,0:T(2,128)} %links.1, ...), custom_call_target="tpu_custom_call" | custom-call | tf_op jit(solution)/shard_map/pallas_call | solution.py:641
  34.5 0.7 %shard_map.114 = (f32[2,20,2,128]{3,2,1,0:T(2,128)}, f32[2,20,2,128]{3,2,1,0:T(2,128)}) custom-call(f32[20,8,128]{2,1,0:T(8,128)S(1)} %get-tuple-element.4.image, f32[20,8,128]{2,1,0:T(8,128)S(1)} %get-tuple-element.5.answer), custom_call_target="tpu_custom_call" | custom-call | tf_op jit(solution)/shard_map/pallas_call | solution.py:691

commit v6 on v5

--- a/solution.py
+++ b/solution.py
@@ -96,12 +96,15 @@
         pl.semaphore_signal(barrier, inc=1, device_id=peer(dx, dy), device_id_type=MESH)
 
     line = [k for k in range(1, n_py) if min(k, n_py - k) <= REACH]
+    line.sort(key=lambda k: -min(k, n_py - k))
     expected = len(line)
+    for k in line[:2]:
+        greet(0, k)
     for dx in (-1, 1):
         for dy in (-1, 1, 0):
             pl.when(inside_grid(dx, dy))(functools.partial(greet, dx, dy))
             expected = expected + jnp.where(inside_grid(dx, dy), 1, 0)
-    for k in line:
+    for k in line[2:]:
         greet(0, k)
     relayed = n_py // 2 > REACH
 
@@ -242,7 +245,8 @@
     ids = lax.broadcasted_iota(I32, (128, 128), 0) & (AGG_DEV - 1)
     hot = [(ids == a).astype(F32) for a in agg_rows]
 
-    received(round1)
+    tiles = round1[:4] + round1[-2:]
+    received(tiles)
 
     def joined(first, size):
         here = jnp.where(core, own[first : first + size], near[first : first + size])
@@ -283,8 +287,9 @@
         axis = shear.ndim - 2
         square = shear * shear
         strain = EPS0 + 0.25 * KZ * (square + turn(square, 4, axis))
-        eta = soft * jnp.exp(jnp.log(strain) * (-1.0 / 3.0))
-        slope = (-2.0 / 3.0 * 0.25 * KZ) * eta / strain * shear
+        log = jnp.log(strain)
+        eta = soft * jnp.exp(log * (-1.0 / 3.0))
+        slope = (-2.0 / 3.0 * 0.25 * KZ) * soft * jnp.exp(log * (-4.0 / 3.0)) * shear
         return eta, slope
 
     def derived(slope, shear):
@@ -306,10 +311,6 @@
         fields += [(x[i], FIELD + 2 * i) for i in range(LAYERS)] + [(rate[0], 2 * LAYERS)]
         return packed(fields, 0, -1)
 
-    halo = (joined(V, LAYERS), joined(X, LAYERS), joined(RATE, 1))
-    rim = (outer(V, LAYERS), outer(X, LAYERS), outer(RATE, 1))
-    here, slope = state(*halo)
-    rim_here, _ = state(*rim)
     edge0, rim_edge0 = edges(0)
     edge1, rim_edge1 = edges(1)
     edge_load, _ = edges(2)
@@ -317,11 +318,19 @@
     rim_at_edge, _ = edge_state(rim_edge0)
     past_edge, _ = edge_state(edge1)
     rim_past_edge, _ = edge_state(rim_edge1)
+    ends_at = [unpacked(e) for e in at_edge]
+    rim_ends_at = [unpacked(e) for e in rim_at_edge]
+
+    received(round1[4:-2])
+    halo = (joined(V, LAYERS), joined(X, LAYERS), joined(RATE, 1))
+    rim = (outer(V, LAYERS), outer(X, LAYERS), outer(RATE, 1))
+    here, slope = state(*halo)
+    rim_here, _ = state(*rim)
     in_edge, _ = edge_state(inside(*halo))
     rim_in_edge, _ = edge_state(inside(*rim))
 
     def triples(states, ends):
-        found = [beside(a, unpacked(e)) for a, e in zip(states, ends)]
+        found = [beside(a, e) for a, e in zip(states, ends)]
         return [tuple(f[i] for f in found) for i in range(3)]
 
     def edge_triples(past, at, within):
@@ -377,8 +386,8 @@
     side, pull, part = coupling(
         halves_of([links_here[k] for k in range(4)]),
         here,
-        triples(here, at_edge),
-        triples(rim_here, rim_at_edge),
+        triples(here, ends_at),
+        triples(rim_here, rim_ends_at),
         True,
     )
     face = (0.5 * KZ) * (eta[:-1] + eta[1:])
@@ -550,16 +559,22 @@
         scale = OMEGA / f[0]
         cols = [c[k] for k in range(4)]
         weights = [f[1 + k] * scale for k in range(4)]
-        operators.append((scale, weights, [a >> 7 for a in cols], [a & 127 for a in cols]))
+        bits = [
+            [((a >> (7 + b)) & 1) == 1 for b in range((n_hi - 1).bit_length())] for a in cols
+        ]
+        operators.append((scale, weights, bits, [a & 127 for a in cols]))
     agg_all = jnp.where(core, own[AGG], near[AGG])
     agg_all = jnp.where(row_ok, agg_all, 0.0).astype(I32)
     sent(round1 + coarse)
+    gathered(0, 0, n_py - 1)
+    for group, (_, ok) in enumerate(pairs):
+        pl.when(ok)(functools.partial(gathered, 1 + group, 0, n_py))
     low = lax.broadcasted_iota(I32, (n_hi, 128), 1) < AGG_DEV
 
     def picked(source, at):
         return jnp.take_along_axis(source, at, axis=1, mode="promise_in_bounds")
 
-    for g, (scale, weights, col_hi, col_lo) in enumerate(operators):
+    for g, (scale, weights, col_bits, col_lo) in enumerate(operators):
         if g == 0:
             gathered(3, 0, n_py)
         else:
@@ -579,10 +594,12 @@
                 ]
                 value = (1.0 - OMEGA) * iterate[c] + target[c]
                 for k in range(4):
-                    found = picked(rows[0], col_lo[k])
-                    for h in range(1, n_hi):
-                        found = jnp.where(col_hi[k] == h, picked(rows[h], col_lo[k]), found)
-                    value = value - weights[k] * found
+                    found = [picked(r, col_lo[k]) for r in rows]
+                    for bit in col_bits[k]:
+                        found = [
+                            jnp.where(bit, b, a) for a, b in zip(found[::2], found[1::2])
+                        ]
+                    value = value - weights[k] * found[0]
                 later.append(value)
             iterate = later
         xs[g, 0] = iterate[0]
@@ -611,9 +628,6 @@
     for d, (dx, dy) in enumerate(OFFSETS):
         result = result + ws[:, d] * turn(corr_beside[dy + 1], -dx, 0)
     ans[...] = result
-    gathered(0, 0, n_py - 1)
-    for group, (_, ok) in enumerate(pairs):
-        pl.when(ok)(functools.partial(gathered, 1 + group, 0, n_py))
 
 
 def write_out(image, answer, image_out, answer_out, sems):

time: 35.6 us -> 35.4 us (level)
  no operation moved by 1% of the time
where the time goes in v6:
time: 35.4 us; the launch traced here: 35.1 us
  Pallas kernels  34.5 us (97%)
  between operations  0.64 us (2%)
    pallas_call x1, Pallas kernels, body(): pl.pallas_call(functools.partial(kernel, n_px, n_py), out_shape=(wide, wi...  33.8 us

profile of v6, /device:TPU:31, one launch (start us, length us, event | category | flops | bytes accessed | tf_op | source)
XLA Modules:
  0.0 35.1 jit_solution(3797007033850066042)
XLA Ops:
  0.6 33.8 %shard_map.113 = (f32[20,8,128]{2,1,0:T(8,128)S(1)}, f32[20,8,128]{2,1,0:T(8,128)S(1)}) custom-call(f32[2,20,2,128]{3,2,1,0:T(2,128)} %velocity.1, f32[2,20,2,128]{3,2,1,0:T(2,128)} %direction.1, f32[2,20,2,128]{3,2,1,0:T(2,128)} %forcing.1, f32[2,128]{1,0:T(2,128)} %softness.1, f32[2,128]{1,0:T(2,128)} %friction.1, s32[4,2,128]{2,1,0:T(2,128)} %links.1, ...), custom_call_target="tpu_custom_call" | custom-call | tf_op jit(solution)/shard_map/pallas_call | solution.py:655
  34.5 0.7 %shard_map.114 = (f32[2,20,2,128]{3,2,1,0:T(2,128)}, f32[2,20,2,128]{3,2,1,0:T(2,128)}) custom-call(f32[20,8,128]{2,1,0:T(8,128)S(1)} %get-tuple-element.4.image, f32[20,8,128]{2,1,0:T(8,128)S(1)} %get-tuple-element.5.answer), custom_call_target="tpu_custom_call" | custom-call | tf_op jit(solution)/shard_map/pallas_call | solution.py:705

commit v7 on v6

--- a/solution.py
+++ b/solution.py
@@ -86,6 +86,11 @@
     def peer(dx, dy):
         return (wrap(px + dx, n_px), wrap(py + dy, n_py))
 
+    odd = lax.rem(px, 2)
+    pairs = []
+    for dx in (1 - 2 * odd, 2 * odd - 1):
+        pairs.append((dx, (px + dx >= 0) & (px + dx < n_px)))
+
     def inside_grid(dx, dy):
         ok = (px >= 0) if dx == 0 else (px > 0) if dx < 0 else (px < n_px - 1)
         return ok if dy == 0 else ok & ((py > 0) if dy < 0 else (py < n_py - 1))
@@ -98,12 +103,14 @@
     line = [k for k in range(1, n_py) if min(k, n_py - k) <= REACH]
     line.sort(key=lambda k: -min(k, n_py - k))
     expected = len(line)
-    for k in line[:2]:
-        greet(0, k)
-    for dx in (-1, 1):
+    for dx, ok in pairs[::-1]:
+        if dx is pairs[0][0]:
+            for k in line[:2]:
+                greet(0, k)
         for dy in (-1, 1, 0):
-            pl.when(inside_grid(dx, dy))(functools.partial(greet, dx, dy))
-            expected = expected + jnp.where(inside_grid(dx, dy), 1, 0)
+            there = ok if dy == 0 else ok & ((py > 0) if dy < 0 else (py < n_py - 1))
+            pl.when(there)(functools.partial(greet, dx, dy))
+            expected = expected + jnp.where(there, 1, 0)
     for k in line[2:]:
         greet(0, k)
     relayed = n_py // 2 > REACH
@@ -199,32 +206,32 @@
     edge_send[1] = packed(moving, 2, 3)
     edge_send[2] = packed([(own[LOAD + i], FIELD + 2 * i) for i in range(LAYERS)], 1, 1)
     pl.semaphore_wait(barrier, expected)
-    if relayed:
-        for k in (REACH, n_py - REACH):
-            pl.semaphore_signal(relay, inc=1, device_id=peer(0, k), device_id_type=MESH)
-    slot = {(dx, dy): 3 * (dy > 0) + dx + 1 for dx in (-1, 0, 1) for dy in (-1, 1)}
     round1 = []
-    def send_round1(src, dst, dx, dy):
-        to_ok, from_ok = inside_grid(dx, dy), inside_grid(-dx, -dy)
-        round1.append(send(src, dst, peer(dx, dy), to_ok, from_ok))
-
-    for dx in (-1, 1):
+
+    def along(dy):
+        return (py >= 0) if dy == 0 else (py > 0) if dy < 0 else (py < n_py - 1)
+
+    for dx, ok in pairs[::-1]:
         for dy in (-1, 1):
-            send_round1(edge_send, edge_recv.at[slot[-dx, -dy]], dx, dy)
-    for c in range(2):
-        low, high = 4 * c + 1, 4 * c + 2
-        for dx, first, second, to in ((1, high, low, 4 * c), (-1, low, high, 4 * c + 3)):
-            there = pl.ds(to, 1)
-            send_round1(own.at[:, pl.ds(first, 1)], near.at[:, there], dx, 0)
-            moved = own.at[pl.ds(0, FAR), pl.ds(second, 1)]
-            send_round1(moved, far.at[:, there], dx, 0)
+            there = edge_recv.at[3 * (dy < 0) + 1 - dx]
+            to_ok, from_ok = ok & along(dy), ok & along(-dy)
+            round1.append(send(edge_send, there, peer(dx, dy), to_ok, from_ok))
+        if relayed and len(round1) == 2:
+            for k in (REACH, n_py - REACH):
+                pl.semaphore_signal(relay, inc=1, device_id=peer(0, k), device_id_type=MESH)
+    for dx, ok in pairs[::-1]:
+        up = lax.div(dx + 1, 2)
+        for c in range(2):
+            there = pl.ds(4 * c + 3 * (1 - up), 1)
+            first, second = pl.ds(4 * c + 1 + up, 1), pl.ds(4 * c + 2 - up, 1)
+            round1.append(send(own.at[:, first], near.at[:, there], peer(dx, 0), ok, ok))
+            moved = own.at[pl.ds(0, FAR), second]
+            round1.append(send(moved, far.at[:, there], peer(dx, 0), ok, ok))
     for dy in (-1, 1):
-        send_round1(edge_send, edge_recv.at[slot[0, -dy]], 0, dy)
-
-    odd = lax.rem(px, 2)
-    pairs = []
-    for dx in (1 - 2 * odd, 2 * odd - 1):
-        pairs.append((dx, (px + dx >= 0) & (px + dx < n_px)))
+        there = edge_recv.at[3 * (dy < 0) + 1]
+        to_ok, from_ok = along(dy), along(-dy)
+        round1.append(send(edge_send, there, peer(0, dy), to_ok, from_ok))
+
     for copy in loads[first_loads:]:
         copy.wait()
     coarse = []

time: 35.4 us -> 35.3 us (level)
  the two profiles are of different devices: /device:TPU:31 before, /device:TPU:32 now
where the time goes in v7:
time: 35.3 us; the launch traced here: 35 us
  Pallas kernels  34.4 us (97%)
  between operations  0.64 us (2%)
    pallas_call x1, Pallas kernels, body(): pl.pallas_call(functools.partial(kernel, n_px, n_py), out_shape=(wide, wi...  33.7 us

profile of v7, /device:TPU:32, one launch (start us, length us, event | category | flops | bytes accessed | tf_op | source)
XLA Modules:
  0.0 35.0 jit_solution(16507884871702171525)
XLA Ops:
  0.6 33.7 %shard_map.113 = (f32[20,8,128]{2,1,0:T(8,128)S(1)}, f32[20,8,128]{2,1,0:T(8,128)S(1)}) custom-call(f32[2,20,2,128]{3,2,1,0:T(2,128)} %velocity.1, f32[2,20,2,128]{3,2,1,0:T(2,128)} %direction.1, f32[2,20,2,128]{3,2,1,0:T(2,128)} %forcing.1, f32[2,128]{1,0:T(2,128)} %softness.1, f32[2,128]{1,0:T(2,128)} %friction.1, s32[4,2,128]{2,1,0:T(2,128)} %links.1, ...), custom_call_target="tpu_custom_call" | custom-call | tf_op jit(solution)/shard_map/pallas_call | solution.py:662
  34.4 0.7 %shard_map.114 = (f32[2,20,2,128]{3,2,1,0:T(2,128)}, f32[2,20,2,128]{3,2,1,0:T(2,128)}) custom-call(f32[20,8,128]{2,1,0:T(8,128)S(1)} %get-tuple-element.4.image, f32[20,8,128]{2,1,0:T(8,128)S(1)} %get-tuple-element.5.answer), custom_call_target="tpu_custom_call" | custom-call | tf_op jit(solution)/shard_map/pallas_call | solution.py:712
